TPU v7x, 32 devices: a whole 2x2x4 slice. The times are simulated.
32 devices in a mesh: gz: 4 (over z), gx: 4 (over y, core), gy: 2 (over x).
Axes of the slice: x: 2, y: 2, z: 4, core: 2. Of those that a mesh axis runs over, the one named last changes fastest.
Arguments:
- fields_in: float32 [6, 16, 256, 256], P(None, 'gz', 'gx', 'gy'), may hold values from -6 to 6
- material: int32 [16, 256, 256], P('gz', 'gx', 'gy'), may hold values from 0 to 3, as said below
- material_eps: float32 [4], replicated, may hold values from 1 to 12
- source_plane: int32 [1], replicated, may hold values from 0 to 15
- source_wave: float32 [4], replicated, may hold values from -8 to 8
- source_profile: float32 [256, 256], P('gx', 'gy'), may hold values from -6 to 6
- forward_fields: bfloat16 [4, 3, 16, 256, 256], P(None, None, 'gz', 'gx', 'gy'), may hold values from -6 to 6
Outputs:
- fields_out: float32 [6, 16, 256, 256], P(None, 'gz', 'gx', 'gy')
- eps_grad: float32 [16, 256, 256], P('gz', 'gx', 'gy')
Inputs may be any that keep to these rules, and one draw needn't show every extreme that they name: `material`: planes z below 6 hold index 1; planes from 10 up hold index 0; the planes between hold 0 or an index of 2 to 3 in each cell.
All inputs are finite; a program needn't handle non-finite values.
Results may differ from a plain program's by a relative error of at most 0.0003.
Values sent between devices are 32-bit elements; how exact they have to be, the bound alone decides.
No kernel may reach another device: no remote copies, remote signals or barrier semaphores. Data moves between devices by JAX's collectives and lax.ppermute only.
A program may use at most 64 MiB of HBM per device.

v0:
```python
import jax
import jax.numpy as jnp
from jax import lax
from jax.sharding import PartitionSpec as P

COURANT = 0.5


def from_behind(block, axis, distance):
    devices = range(lax.axis_size(axis))
    route = [(i - distance, i) for i in devices if i - distance in devices]
    return lax.ppermute(block, axis, route)


def passed_along(array, axis, by):
    length = lax.axis_size(axis)
    return lax.ppermute(array, axis, [(i, (i + by) % length) for i in range(length)])


def z_neighbour(planes, offset):
    if offset < 0:
        border = planes[:, :1]
    else:
        border = planes[:, -1:]
    arrived = from_behind(border, "gz", offset)
    if offset < 0:
        return jnp.concatenate([planes[:, 1:], arrived], axis=1)
    return jnp.concatenate([arrived, planes[:, :-1]], axis=1)


def x_neighbour(planes, offset):
    if offset < 0:
        border = planes[:, :, :1]
    else:
        border = planes[:, :, -1:]
    arrived = passed_along(border, "gx", offset)
    if offset < 0:
        return jnp.concatenate([planes[:, :, 1:], arrived], axis=2)
    return jnp.concatenate([arrived, planes[:, :, :-1]], axis=2)


def y_neighbour(planes, offset):
    if offset < 0:
        border = planes[:, :, :, :1]
    else:
        border = planes[:, :, :, -1:]
    arrived = passed_along(border, "gy", offset)
    if offset < 0:
        return jnp.concatenate([planes[:, :, :, 1:], arrived], axis=3)
    return jnp.concatenate([arrived, planes[:, :, :, :-1]], axis=3)


def yee_step(electric, magnetic, coef, source, amplitude, z_side, x_side, y_side):
    elec_x, elec_y, elec_z = (electric[0], electric[1], electric[2])
    z_next = z_side(jnp.stack([elec_x, elec_y]), -1)
    x_next = x_side(jnp.stack([elec_y, elec_z]), -1)
    y_next = y_side(jnp.stack([elec_x, elec_z]), -1)
    curl_x = y_next[1] - elec_z - (z_next[1] - elec_y)
    curl_y = z_next[0] - elec_x - (x_next[1] - elec_z)
    curl_z = x_next[0] - elec_y - (y_next[0] - elec_x)
    magn_x = magnetic[0] - COURANT * curl_x
    magn_y = magnetic[1] - COURANT * curl_y
    magn_z = magnetic[2] - COURANT * curl_z
    z_prev = z_side(jnp.stack([magn_x, magn_y]), 1)
    x_prev = x_side(jnp.stack([magn_y, magn_z]), 1)
    y_prev = y_side(jnp.stack([magn_x, magn_z]), 1)
    back_x = magn_z - y_prev[1] - (magn_y - z_prev[1])
    back_y = magn_x - z_prev[0] - (magn_z - x_prev[1])
    back_z = magn_y - x_prev[0] - (magn_x - y_prev[0])
    new_x = elec_x + coef * back_x + coef * amplitude * source
    new_y = elec_y + coef * back_y
    new_z = elec_z + coef * back_z
    return (jnp.stack([new_x, new_y, new_z]), jnp.stack([magn_x, magn_y, magn_z]))


def accumulate(grad, stored, electric):
    stored = stored.astype(jnp.float32)
    return grad + stored[0] * electric[0] + stored[1] * electric[1] + stored[2] * electric[2]


def on_device(
    fields_in, material, material_eps, source_plane, source_wave, source_profile, forward_fields
):
    depth, width_x, width_y = material.shape
    permit = jnp.zeros(material.shape, jnp.float32)
    for which in range(material_eps.shape[0]):
        permit = permit + jnp.where(material == which, material_eps[which], 0.0)
    coef = COURANT / permit
    zpos = lax.axis_index("gz") * depth + jnp.arange(depth)
    source = (
        jnp.where(zpos == source_plane[0], 1.0, 0.0).astype(jnp.float32)[:, None, None]
        * source_profile[None]
    )
    count = source_wave.shape[0]
    grad = jnp.zeros(material.shape, jnp.float32)
    stacked = jnp.concatenate([fields_in, coef[None], source[None]], axis=0)
    electric = stacked[0:3]
    magnetic = stacked[3:6]
    wide_coef = stacked[6]
    wide_source = stacked[7]
    for instant in range(count):
        electric, magnetic = yee_step(
            electric,
            magnetic,
            wide_coef,
            wide_source,
            source_wave[instant],
            z_neighbour,
            x_neighbour,
            y_neighbour,
        )
        grad = accumulate(grad, forward_fields[instant], electric)
    fields_out = jnp.concatenate([electric, magnetic], axis=0)
    eps_grad = jnp.where(material >= 2, -grad, 0.0)
    return (fields_out, eps_grad)


def solution(mesh):
    placed = (
        P(None, "gz", "gx", "gy"),
        P("gz", "gx", "gy"),
        P(),
        P(),
        P(),
        P("gx", "gy"),
        P(None, None, "gz", "gx", "gy"),
    )
    return jax.shard_map(
        on_device,
        mesh=mesh,
        in_specs=placed,
        out_specs=(P(None, "gz", "gx", "gy"), P("gz", "gx", "gy")),
        check_vma=False,
    )
```

profile of v0, /device:TPU:0, one launch (start us, length us, event | category | flops | bytes accessed | tf_op | source)
XLA Modules:
  0.0 132.3 jit_solution(11749388981878146393)
XLA Ops:
  1.5 2.4 %collective-permute-start = (f32[2,4,1,128]{3,2,1,0:T(1,128)S(1)}, f32[2,4,1,128]{3,2,1,0:T(1,128)S(1)}, u32[]{:S(2)}, u32[]{:S(2)}) collective-permute-start(f32[2,4,1,128]{3,2,1,0:T(1,128)S(1)} %slice.411), channel_id=1, source_target_pairs={{0,6},{2,0},{4,2},{6,4},{1,7},{3,1},{5,3},{7,5},{8,14},{10,8},{12,... | collective-permute-start | bytes 12296 | tf_op jit(solution)/shard_map/ppermute | solution.py:17
  13.3 5.9 %collective-permute-done.1 = f32[2,4,64,1]{3,2,1,0:T(8,128)S(1)} collective-permute-done((f32[2,4,64,1]{3,2,1,0:T(8,128)S(1)}, f32[2,4,64,1]{3,2,1,0:T(8,128)S(1)}, u32[]{:S(2)}, u32[]{:S(2)}) %collective-permute-start.1) | collective-permute-done | bytes 2080 | tf_op jit(solution)/shard_map/ppermute | solution.py:17
  19.6 4.4 %collective-permute-start.4 = (f32[2,1,64,128]{3,2,1,0:T(8,128)S(1)}, f32[2,1,64,128]{3,2,1,0:T(8,128)S(1)}, u32[]{:S(2)}, u32[]{:S(2)}) collective-permute-start(f32[2,1,64,128]{3,2,1,0:T(8,128)S(1)} %fusion.201), channel_id=1, source_target_pairs={{0,8},{8,16},{16,24},{1,9},{9,17},{17,25},{2,10},{10,18},{18,26},{... | collective-permute-start | bytes 196616 | tf_op jit(solution)/shard_map/ppermute | solution.py:12
  24.0 1.7 %collective-permute-start.3 = (f32[2,4,64,1]{3,2,1,0:T(8,128)S(1)}, f32[2,4,64,1]{3,2,1,0:T(8,128)S(1)}, u32[]{:S(2)}, u32[]{:S(2)}) collective-permute-start(f32[2,4,64,1]{3,2,1,0:T(8,128)S(1)} %fusion.3), channel_id=1, source_target_pairs={{0,1},{1,0},{2,3},{3,2},{4,5},{5,4},{6,7},{7,6},{8,9},{9,8},{10,11... | collective-permute-start | bytes 6152 | tf_op jit(solution)/shard_map/ppermute | solution.py:17
  25.7 7.1 %collective-permute-done.3 = f32[2,4,64,1]{3,2,1,0:T(8,128)S(1)} collective-permute-done((f32[2,4,64,1]{3,2,1,0:T(8,128)S(1)}, f32[2,4,64,1]{3,2,1,0:T(8,128)S(1)}, u32[]{:S(2)}, u32[]{:S(2)}) %collective-permute-start.3) | collective-permute-done | bytes 2080 | tf_op jit(solution)/shard_map/ppermute | solution.py:17
  32.9 2.7 %fusion.182 = (f32[4,64,128]{2,1,0:T(8,128)S(1)}, f32[4,64,128]{2,1,0:T(8,128)S(1)}, f32[4,64,128]{2,1,0:T(8,128)S(1)}) fusion(f32[2,4,64,128]{3,2,1,0:T(8,128)S(1)} %get-tuple-element.45, f32[2,4,64,128]{3,2,1,0:T(8,128)S(1)} %get-tuple-element.44, f32[6,4,64,128]{3,2,1,0:T(8,128)S(1)} %copy-done, f32[]{:T(128)} %bitcast.4, ...), kind=kLoop, calls=%fused_computation.312 | loop fusion | flops 983040 | bytes 2359312 | tf_op jit(solution)/shard_map/add | solution.py:71
  35.6 2.6 %fusion.177 = (f32[4,64,128]{2,1,0:T(8,128)S(1)}, f32[4,64,128]{2,1,0:T(8,128)S(1)}) fusion(f32[4,64,128]{2,1,0:T(8,128)S(1)} %get-tuple-element.7, f32[2,4,64,128]{3,2,1,0:T(8,128)S(1)} %get-tuple-element.43, f32[2,4,64,128]{3,2,1,0:T(8,128)S(1)} %get-tuple-element.45, f32[6,4,64,128]{3,2,1,0:T(8,128)S(1)} %copy-done, f32[]{:T(128)} %bitcast.4, ...), kind=kLoop, calls=%fused_computation.305 | loop fusion | flops 786432 | bytes 1703952 | tf_op jit(solution)/shard_map/add | solution.py:72
  39.0 3.2 %fusion.73 = f32[4,64,128]{2,1,0:T(8,128)S(1)} fusion(f32[4,64,128]{2,1,0:T(8,128)S(1)} %get-tuple-element.10, f32[2,4,64,128]{3,2,1,0:T(8,128)S(1)} %get-tuple-element.44, f32[4,64,128]{2,1,0:T(8,128)S(1)} %get-tuple-element.8, f32[2,4,64,128]{3,2,1,0:T(8,128)S(1)} %get-tuple-element.43, f32[64,128]{1,0:T(8,128)S(1)} %copy-done.3, ...), kind=kLoop, calls=%fused_computation.161 | loop fusion | flops 688128 | bytes 950308 | tf_op jit(solution)/shard_map/add | solution.py:70
  44.0 1.9 %collective-permute-start.7 = (f32[2,4,64,1]{3,2,1,0:T(8,128)S(1)}, f32[2,4,64,1]{3,2,1,0:T(8,128)S(1)}, u32[]{:S(2)}, u32[]{:S(2)}) collective-permute-start(f32[2,4,64,1]{3,2,1,0:T(8,128)S(1)} %pad_maximum_fusion.11), channel_id=1, source_target_pairs={{0,1},{1,0},{2,3},{3,2},{4,5},{5,4},{6,7},{7,6},{8,9},{9,8},{10,11... | collective-permute-start | bytes 6152 | tf_op jit(solution)/shard_map/ppermute | solution.py:17
  45.9 6.7 %collective-permute-done.7 = f32[2,4,64,1]{3,2,1,0:T(8,128)S(1)} collective-permute-done((f32[2,4,64,1]{3,2,1,0:T(8,128)S(1)}, f32[2,4,64,1]{3,2,1,0:T(8,128)S(1)}, u32[]{:S(2)}, u32[]{:S(2)}) %collective-permute-start.7) | collective-permute-done | bytes 2080 | tf_op jit(solution)/shard_map/ppermute | solution.py:17
  52.9 4.4 %collective-permute-start.10 = (f32[2,1,64,128]{3,2,1,0:T(8,128)S(1)}, f32[2,1,64,128]{3,2,1,0:T(8,128)S(1)}, u32[]{:S(2)}, u32[]{:S(2)}) collective-permute-start(f32[2,1,64,128]{3,2,1,0:T(8,128)S(1)} %fusion.200), channel_id=1, source_target_pairs={{0,8},{8,16},{16,24},{1,9},{9,17},{17,25},{2,10},{10,18},{18,26},{... | collective-permute-start | bytes 196616 | tf_op jit(solution)/shard_map/ppermute | solution.py:12
  57.4 1.7 %collective-permute-start.9 = (f32[2,4,64,1]{3,2,1,0:T(8,128)S(1)}, f32[2,4,64,1]{3,2,1,0:T(8,128)S(1)}, u32[]{:S(2)}, u32[]{:S(2)}) collective-permute-start(f32[2,4,64,1]{3,2,1,0:T(8,128)S(1)} %fusion.2), channel_id=1, source_target_pairs={{0,1},{1,0},{2,3},{3,2},{4,5},{5,4},{6,7},{7,6},{8,9},{9,8},{10,11... | collective-permute-start | bytes 6152 | tf_op jit(solution)/shard_map/ppermute | solution.py:17
  59.2 7.5 %collective-permute-done.9 = f32[2,4,64,1]{3,2,1,0:T(8,128)S(1)} collective-permute-done((f32[2,4,64,1]{3,2,1,0:T(8,128)S(1)}, f32[2,4,64,1]{3,2,1,0:T(8,128)S(1)}, u32[]{:S(2)}, u32[]{:S(2)}) %collective-permute-start.9) | collective-permute-done | bytes 2080 | tf_op jit(solution)/shard_map/ppermute | solution.py:17
  66.8 2.6 %fusion.153 = f32[4,64,128]{2,1,0:T(8,128)S(1)} fusion(f32[4,64,128]{2,1,0:T(8,128)S(1)} %get-tuple-element.9, f32[4,64,128]{2,1,0:T(8,128)S(1)} %get-tuple-element.28, f32[2,4,64,128]{3,2,1,0:T(8,128)S(1)} %get-tuple-element.41, f32[4,64,128]{2,1,0:T(8,128)S(1)} %get-tuple-element.29, f32[2,4,64,128]{3,2,1,0:T(8,128)S(1)} %get-tuple-element.42, ...), kind=kLoop, calls=%fused_computation.272 | loop fusion | flops 557056 | bytes 917520 | tf_op jit(solution)/shard_map/add | solution.py:72
  69.4 3.3 %fusion.74 = (f32[4,64,128]{2,1,0:T(8,128)S(1)}, f32[4,64,128]{2,1,0:T(8,128)S(1)}) fusion(f32[4,64,128]{2,1,0:T(8,128)S(1)} %fusion.73, f32[4,64,128]{2,1,0:T(8,128)S(1)} %get-tuple-element.29, f32[2,4,64,128]{3,2,1,0:T(8,128)S(1)} %get-tuple-element.40, f32[4,64,128]{2,1,0:T(8,128)S(1)} %get-tuple-element.27, f32[2,4,64,128]{3,2,1,0:T(8,128)S(1)} %get-tuple-element.41, ...), kind=kLoop, calls=%fused_computation.162 | loop fusion | flops 851968 | bytes 1605668 | tf_op jit(solution)/shard_map/add | solution.py:70
  76.3 6.7 %collective-permute-done.13 = f32[2,4,64,1]{3,2,1,0:T(8,128)S(1)} collective-permute-done((f32[2,4,64,1]{3,2,1,0:T(8,128)S(1)}, f32[2,4,64,1]{3,2,1,0:T(8,128)S(1)}, u32[]{:S(2)}, u32[]{:S(2)}) %collective-permute-start.13) | collective-permute-done | bytes 2080 | tf_op jit(solution)/shard_map/ppermute | solution.py:17
  83.3 4.3 %collective-permute-start.16 = (f32[2,1,64,128]{3,2,1,0:T(8,128)S(1)}, f32[2,1,64,128]{3,2,1,0:T(8,128)S(1)}, u32[]{:S(2)}, u32[]{:S(2)}) collective-permute-start(f32[2,1,64,128]{3,2,1,0:T(8,128)S(1)} %fusion.199), channel_id=1, source_target_pairs={{0,8},{8,16},{16,24},{1,9},{9,17},{17,25},{2,10},{10,18},{18,26},{... | collective-permute-start | bytes 196616 | tf_op jit(solution)/shard_map/ppermute | solution.py:12
  89.4 7.3 %collective-permute-done.15 = f32[2,4,64,1]{3,2,1,0:T(8,128)S(1)} collective-permute-done((f32[2,4,64,1]{3,2,1,0:T(8,128)S(1)}, f32[2,4,64,1]{3,2,1,0:T(8,128)S(1)}, u32[]{:S(2)}, u32[]{:S(2)}) %collective-permute-start.15) | collective-permute-done | bytes 2080 | tf_op jit(solution)/shard_map/ppermute | solution.py:17
  96.9 2.6 %fusion.129 = f32[4,64,128]{2,1,0:T(8,128)S(1)} fusion(f32[4,64,128]{2,1,0:T(8,128)S(1)} %fusion.153, f32[4,64,128]{2,1,0:T(8,128)S(1)} %get-tuple-element.25, f32[2,4,64,128]{3,2,1,0:T(8,128)S(1)} %get-tuple-element.38, f32[4,64,128]{2,1,0:T(8,128)S(1)} %get-tuple-element.26, f32[2,4,64,128]{3,2,1,0:T(8,128)S(1)} %get-tuple-element.39, f32[]{:T(128)} %bitcast.4, ...), kind=kLoop, calls=%fused_computation.239 | loop fusion | flops 557056 | bytes 917520 | tf_op jit(solution)/shard_map/add | solution.py:72
  99.4 3.3 %fusion.75 = (f32[4,64,128]{2,1,0:T(8,128)S(1)}, f32[4,64,128]{2,1,0:T(8,128)S(1)}) fusion(f32[4,64,128]{2,1,0:T(8,128)S(1)} %get-tuple-element.32, f32[4,64,128]{2,1,0:T(8,128)S(1)} %get-tuple-element.26, f32[2,4,64,128]{3,2,1,0:T(8,128)S(1)} %get-tuple-element.37, f32[4,64,128]{2,1,0:T(8,128)S(1)} %get-tuple-element.24, ...), kind=kLoop, calls=%fused_computation.163 | loop fusion | flops 851968 | bytes 1605668 | tf_op jit(solution)/shard_map/add | solution.py:70
  106.8 6.2 %collective-permute-done.19 = f32[2,4,64,1]{3,2,1,0:T(8,128)S(1)} collective-permute-done((f32[2,4,64,1]{3,2,1,0:T(8,128)S(1)}, f32[2,4,64,1]{3,2,1,0:T(8,128)S(1)}, u32[]{:S(2)}, u32[]{:S(2)}) %collective-permute-start.19) | collective-permute-done | bytes 2080 | tf_op jit(solution)/shard_map/ppermute | solution.py:17
  113.5 4.3 %collective-permute-start.22 = (f32[2,1,64,128]{3,2,1,0:T(8,128)S(1)}, f32[2,1,64,128]{3,2,1,0:T(8,128)S(1)}, u32[]{:S(2)}, u32[]{:S(2)}) collective-permute-start(f32[2,1,64,128]{3,2,1,0:T(8,128)S(1)} %fusion.198), channel_id=1, source_target_pairs={{0,8},{8,16},{16,24},{1,9},{9,17},{17,25},{2,10},{10,18},{18,26},{... | collective-permute-start | bytes 196616 | tf_op jit(solution)/shard_map/ppermute | solution.py:12
  119.7 7.3 %collective-permute-done.21 = f32[2,4,64,1]{3,2,1,0:T(8,128)S(1)} collective-permute-done((f32[2,4,64,1]{3,2,1,0:T(8,128)S(1)}, f32[2,4,64,1]{3,2,1,0:T(8,128)S(1)}, u32[]{:S(2)}, u32[]{:S(2)}) %collective-permute-start.21) | collective-permute-done | bytes 2080 | tf_op jit(solution)/shard_map/ppermute | solution.py:17
  127.2 4.2 %fusion.80 = (f32[4,64,128]{2,1,0:T(8,128)}, f32[4,64,128]{2,1,0:T(8,128)S(1)}, f32[4,64,128]{2,1,0:T(8,128)S(1)}, f32[4,64,128]{2,1,0:T(8,128)S(1)}) fusion(f32[1,3,4,64,128]{4,3,2,1,0:T(8,128)S(1)} %get-tuple-element.16, f32[4,64,128]{2,1,0:T(8,128)S(1)} %fusion.129, f32[1,3,4,64,128]{4,3,2,1,0:T(8,128)S(1)} %get-tuple-element.17, ...), kind=kLoop, calls=%fused_computation.169 | loop fusion | flops 1867776 | bytes 4620324 | tf_op jit(solution)/shard_map/jit(_where)/select_n | solution.py:114
  (97 shorter events, 26.4 us)
Async XLA Ops:
  1.5 10.0 %collective-permute-start = (f32[2,4,1,128]{3,2,1,0:T(1,128)S(1)}, f32[2,4,1,128]{3,2,1,0:T(1,128)S(1)}, u32[]{:S(2)}, u32[]{:S(2)}) collective-permute-start(f32[2,4,1,128]{3,2,1,0:T(1,128)S(1)} %slice.411), channel_id=1, source_target_pairs={{0,6},{2,0},{4,2},{6,4},{1,7},{3,1},{5,3},{7,5},{8,14},{10,8},{12,... | collective-permute-start | bytes 12296 | tf_op jit(solution)/shard_map/ppermute | solution.py:17
  4.7 6.8 %collective-permute-start.2 = (f32[2,1,64,128]{3,2,1,0:T(8,128)S(1)}, f32[2,1,64,128]{3,2,1,0:T(8,128)S(1)}, u32[]{:S(2)}, u32[]{:S(2)}) collective-permute-start(f32[2,1,64,128]{3,2,1,0:T(8,128)S(1)} %slice.421), channel_id=1, source_target_pairs={{8,0},{16,8},{24,16},{9,1},{17,9},{25,17},{10,2},{18,10},{26,18},{... | collective-permute-start | bytes 196616 | tf_op jit(solution)/shard_map/ppermute | solution.py:12
  11.6 7.6 %collective-permute-start.1 = (f32[2,4,64,1]{3,2,1,0:T(8,128)S(1)}, f32[2,4,64,1]{3,2,1,0:T(8,128)S(1)}, u32[]{:S(2)}, u32[]{:S(2)}) collective-permute-start(f32[2,4,64,1]{3,2,1,0:T(8,128)S(1)} %pad_maximum_fusion.15), channel_id=1, source_target_pairs={{0,1},{1,0},{2,3},{3,2},{4,5},{5,4},{6,7},{7,6},{8,9},{9,8},{10,11... | collective-permute-start | bytes 6152 | tf_op jit(solution)/shard_map/ppermute | solution.py:17
  19.5 13.2 %collective-permute-start.5 = (f32[2,4,1,128]{3,2,1,0:T(1,128)S(1)}, f32[2,4,1,128]{3,2,1,0:T(1,128)S(1)}, u32[]{:S(2)}, u32[]{:S(2)}) collective-permute-start(f32[2,4,1,128]{3,2,1,0:T(1,128)S(1)} %fusion.205), channel_id=1, source_target_pairs={{0,2},{2,4},{4,6},{6,0},{1,3},{3,5},{5,7},{7,1},{8,10},{10,12},{12... | collective-permute-start | bytes 12296 | tf_op jit(solution)/shard_map/ppermute | solution.py:17
  19.6 13.2 %collective-permute-start.4 = (f32[2,1,64,128]{3,2,1,0:T(8,128)S(1)}, f32[2,1,64,128]{3,2,1,0:T(8,128)S(1)}, u32[]{:S(2)}, u32[]{:S(2)}) collective-permute-start(f32[2,1,64,128]{3,2,1,0:T(8,128)S(1)} %fusion.201), channel_id=1, source_target_pairs={{0,8},{8,16},{16,24},{1,9},{9,17},{17,25},{2,10},{10,18},{18,26},{... | collective-permute-start | bytes 196616 | tf_op jit(solution)/shard_map/ppermute | solution.py:12
  24.0 8.8 %collective-permute-start.3 = (f32[2,4,64,1]{3,2,1,0:T(8,128)S(1)}, f32[2,4,64,1]{3,2,1,0:T(8,128)S(1)}, u32[]{:S(2)}, u32[]{:S(2)}) collective-permute-start(f32[2,4,64,1]{3,2,1,0:T(8,128)S(1)} %fusion.3), channel_id=1, source_target_pairs={{0,1},{1,0},{2,3},{3,2},{4,5},{5,4},{6,7},{7,6},{8,9},{9,8},{10,11... | collective-permute-start | bytes 6152 | tf_op jit(solution)/shard_map/ppermute | solution.py:17
  42.4 10.2 %collective-permute-start.6 = (f32[2,4,1,128]{3,2,1,0:T(1,128)S(1)}, f32[2,4,1,128]{3,2,1,0:T(1,128)S(1)}, u32[]{:S(2)}, u32[]{:S(2)}) collective-permute-start(f32[2,4,1,128]{3,2,1,0:T(1,128)S(1)} %pad_maximum_fusion.33), channel_id=1, source_target_pairs={{0,6},{2,0},{4,2},{6,4},{1,7},{3,1},{5,3},{7,5},{8,14},{10,8},{12,... | collective-permute-start | bytes 12296 | tf_op jit(solution)/shard_map/ppermute | solution.py:17
  42.7 9.9 %collective-permute-start.8 = (f32[2,1,64,128]{3,2,1,0:T(8,128)S(1)}, f32[2,1,64,128]{3,2,1,0:T(8,128)S(1)}, u32[]{:S(2)}, u32[]{:S(2)}) collective-permute-start(f32[2,1,64,128]{3,2,1,0:T(8,128)S(1)} %pad_maximum_fusion.30), channel_id=1, source_target_pairs={{8,0},{16,8},{24,16},{9,1},{17,9},{25,17},{10,2},{18,10},{26,18},{... | collective-permute-start | bytes 196616 | tf_op jit(solution)/shard_map/ppermute | solution.py:12
  44.0 8.6 %collective-permute-start.7 = (f32[2,4,64,1]{3,2,1,0:T(8,128)S(1)}, f32[2,4,64,1]{3,2,1,0:T(8,128)S(1)}, u32[]{:S(2)}, u32[]{:S(2)}) collective-permute-start(f32[2,4,64,1]{3,2,1,0:T(8,128)S(1)} %pad_maximum_fusion.11), channel_id=1, source_target_pairs={{0,1},{1,0},{2,3},{3,2},{4,5},{5,4},{6,7},{7,6},{8,9},{9,8},{10,11... | collective-permute-start | bytes 6152 | tf_op jit(solution)/shard_map/ppermute | solution.py:17
  52.9 13.8 %collective-permute-start.11 = (f32[2,4,1,128]{3,2,1,0:T(1,128)S(1)}, f32[2,4,1,128]{3,2,1,0:T(1,128)S(1)}, u32[]{:S(2)}, u32[]{:S(2)}) collective-permute-start(f32[2,4,1,128]{3,2,1,0:T(1,128)S(1)} %fusion.204), channel_id=1, source_target_pairs={{0,2},{2,4},{4,6},{6,0},{1,3},{3,5},{5,7},{7,1},{8,10},{10,12},{12... | collective-permute-start | bytes 12296 | tf_op jit(solution)/shard_map/ppermute | solution.py:17
  52.9 13.7 %collective-permute-start.10 = (f32[2,1,64,128]{3,2,1,0:T(8,128)S(1)}, f32[2,1,64,128]{3,2,1,0:T(8,128)S(1)}, u32[]{:S(2)}, u32[]{:S(2)}) collective-permute-start(f32[2,1,64,128]{3,2,1,0:T(8,128)S(1)} %fusion.200), channel_id=1, source_target_pairs={{0,8},{8,16},{16,24},{1,9},{9,17},{17,25},{2,10},{10,18},{18,26},{... | collective-permute-start | bytes 196616 | tf_op jit(solution)/shard_map/ppermute | solution.py:12
  57.4 9.2 %collective-permute-start.9 = (f32[2,4,64,1]{3,2,1,0:T(8,128)S(1)}, f32[2,4,64,1]{3,2,1,0:T(8,128)S(1)}, u32[]{:S(2)}, u32[]{:S(2)}) collective-permute-start(f32[2,4,64,1]{3,2,1,0:T(8,128)S(1)} %fusion.2), channel_id=1, source_target_pairs={{0,1},{1,0},{2,3},{3,2},{4,5},{5,4},{6,7},{7,6},{8,9},{9,8},{10,11... | collective-permute-start | bytes 6152 | tf_op jit(solution)/shard_map/ppermute | solution.py:17
  72.9 10.1 %collective-permute-start.12 = (f32[2,4,1,128]{3,2,1,0:T(1,128)S(1)}, f32[2,4,1,128]{3,2,1,0:T(1,128)S(1)}, u32[]{:S(2)}, u32[]{:S(2)}) collective-permute-start(f32[2,4,1,128]{3,2,1,0:T(1,128)S(1)} %pad_maximum_fusion.32), channel_id=1, source_target_pairs={{0,6},{2,0},{4,2},{6,4},{1,7},{3,1},{5,3},{7,5},{8,14},{10,8},{12,... | collective-permute-start | bytes 12296 | tf_op jit(solution)/shard_map/ppermute | solution.py:17
  73.3 9.7 %collective-permute-start.14 = (f32[2,1,64,128]{3,2,1,0:T(8,128)S(1)}, f32[2,1,64,128]{3,2,1,0:T(8,128)S(1)}, u32[]{:S(2)}, u32[]{:S(2)}) collective-permute-start(f32[2,1,64,128]{3,2,1,0:T(8,128)S(1)} %pad_maximum_fusion.29), channel_id=1, source_target_pairs={{8,0},{16,8},{24,16},{9,1},{17,9},{25,17},{10,2},{18,10},{26,18},{... | collective-permute-start | bytes 196616 | tf_op jit(solution)/shard_map/ppermute | solution.py:12
  74.6 8.5 %collective-permute-start.13 = (f32[2,4,64,1]{3,2,1,0:T(8,128)S(1)}, f32[2,4,64,1]{3,2,1,0:T(8,128)S(1)}, u32[]{:S(2)}, u32[]{:S(2)}) collective-permute-start(f32[2,4,64,1]{3,2,1,0:T(8,128)S(1)} %pad_maximum_fusion.7), channel_id=1, source_target_pairs={{0,1},{1,0},{2,3},{3,2},{4,5},{5,4},{6,7},{7,6},{8,9},{9,8},{10,11... | collective-permute-start | bytes 6152 | tf_op jit(solution)/shard_map/ppermute | solution.py:17
  83.2 13.5 %collective-permute-start.17 = (f32[2,4,1,128]{3,2,1,0:T(1,128)S(1)}, f32[2,4,1,128]{3,2,1,0:T(1,128)S(1)}, u32[]{:S(2)}, u32[]{:S(2)}) collective-permute-start(f32[2,4,1,128]{3,2,1,0:T(1,128)S(1)} %fusion.203), channel_id=1, source_target_pairs={{0,2},{2,4},{4,6},{6,0},{1,3},{3,5},{5,7},{7,1},{8,10},{10,12},{12... | collective-permute-start | bytes 12296 | tf_op jit(solution)/shard_map/ppermute | solution.py:17
  83.3 13.4 %collective-permute-start.16 = (f32[2,1,64,128]{3,2,1,0:T(8,128)S(1)}, f32[2,1,64,128]{3,2,1,0:T(8,128)S(1)}, u32[]{:S(2)}, u32[]{:S(2)}) collective-permute-start(f32[2,1,64,128]{3,2,1,0:T(8,128)S(1)} %fusion.199), channel_id=1, source_target_pairs={{0,8},{8,16},{16,24},{1,9},{9,17},{17,25},{2,10},{10,18},{18,26},{... | collective-permute-start | bytes 196616 | tf_op jit(solution)/shard_map/ppermute | solution.py:12
  87.7 9.0 %collective-permute-start.15 = (f32[2,4,64,1]{3,2,1,0:T(8,128)S(1)}, f32[2,4,64,1]{3,2,1,0:T(8,128)S(1)}, u32[]{:S(2)}, u32[]{:S(2)}) collective-permute-start(f32[2,4,64,1]{3,2,1,0:T(8,128)S(1)} %fusion.1), channel_id=1, source_target_pairs={{0,1},{1,0},{2,3},{3,2},{4,5},{5,4},{6,7},{7,6},{8,9},{9,8},{10,11... | collective-permute-start | bytes 6152 | tf_op jit(solution)/shard_map/ppermute | solution.py:17
  102.9 10.1 %collective-permute-start.18 = (f32[2,4,1,128]{3,2,1,0:T(1,128)S(1)}, f32[2,4,1,128]{3,2,1,0:T(1,128)S(1)}, u32[]{:S(2)}, u32[]{:S(2)}) collective-permute-start(f32[2,4,1,128]{3,2,1,0:T(1,128)S(1)} %pad_maximum_fusion.31), channel_id=1, source_target_pairs={{0,6},{2,0},{4,2},{6,4},{1,7},{3,1},{5,3},{7,5},{8,14},{10,8},{12,... | collective-permute-start | bytes 12296 | tf_op jit(solution)/shard_map/ppermute | solution.py:17
  103.8 9.3 %collective-permute-start.20 = (f32[2,1,64,128]{3,2,1,0:T(8,128)S(1)}, f32[2,1,64,128]{3,2,1,0:T(8,128)S(1)}, u32[]{:S(2)}, u32[]{:S(2)}) collective-permute-start(f32[2,1,64,128]{3,2,1,0:T(8,128)S(1)} %pad_maximum_fusion.28), channel_id=1, source_target_pairs={{8,0},{16,8},{24,16},{9,1},{17,9},{25,17},{10,2},{18,10},{26,18},{... | collective-permute-start | bytes 196616 | tf_op jit(solution)/shard_map/ppermute | solution.py:12
  105.1 8.0 %collective-permute-start.19 = (f32[2,4,64,1]{3,2,1,0:T(8,128)S(1)}, f32[2,4,64,1]{3,2,1,0:T(8,128)S(1)}, u32[]{:S(2)}, u32[]{:S(2)}) collective-permute-start(f32[2,4,64,1]{3,2,1,0:T(8,128)S(1)} %pad_maximum_fusion.3), channel_id=1, source_target_pairs={{0,1},{1,0},{2,3},{3,2},{4,5},{5,4},{6,7},{7,6},{8,9},{9,8},{10,11... | collective-permute-start | bytes 6152 | tf_op jit(solution)/shard_map/ppermute | solution.py:17
  113.4 13.6 %collective-permute-start.23 = (f32[2,4,1,128]{3,2,1,0:T(1,128)S(1)}, f32[2,4,1,128]{3,2,1,0:T(1,128)S(1)}, u32[]{:S(2)}, u32[]{:S(2)}) collective-permute-start(f32[2,4,1,128]{3,2,1,0:T(1,128)S(1)} %fusion.202), channel_id=1, source_target_pairs={{0,2},{2,4},{4,6},{6,0},{1,3},{3,5},{5,7},{7,1},{8,10},{10,12},{12... | collective-permute-start | bytes 12296 | tf_op jit(solution)/shard_map/ppermute | solution.py:17
  113.5 13.5 %collective-permute-start.22 = (f32[2,1,64,128]{3,2,1,0:T(8,128)S(1)}, f32[2,1,64,128]{3,2,1,0:T(8,128)S(1)}, u32[]{:S(2)}, u32[]{:S(2)}) collective-permute-start(f32[2,1,64,128]{3,2,1,0:T(8,128)S(1)} %fusion.198), channel_id=1, source_target_pairs={{0,8},{8,16},{16,24},{1,9},{9,17},{17,25},{2,10},{10,18},{18,26},{... | collective-permute-start | bytes 196616 | tf_op jit(solution)/shard_map/ppermute | solution.py:12
  117.8 9.2 %collective-permute-start.21 = (f32[2,4,64,1]{3,2,1,0:T(8,128)S(1)}, f32[2,4,64,1]{3,2,1,0:T(8,128)S(1)}, u32[]{:S(2)}, u32[]{:S(2)}) collective-permute-start(f32[2,4,64,1]{3,2,1,0:T(8,128)S(1)} %fusion), channel_id=1, source_target_pairs={{0,1},{1,0},{2,3},{3,2},{4,5},{5,4},{6,7},{7,6},{8,9},{9,8},{10,11... | collective-permute-start | bytes 6152 | tf_op jit(solution)/shard_map/ppermute | solution.py:17
  (5 other events, 26.0 us)
where the time goes:
time: 133 us; the launch traced here: 132 us
  waiting for transfers between devices  54.8 us (41%)
  starting transfers between devices  40.3 us (30%)
  other arithmetic  27.2 us (20%)
  local copies, waits for them, and re-layouts  8.2 us (6%)
  between operations  1.82 us (1%)
    ppermute x16, waiting for transfers between devices, passed_along(): lax.ppermute(array, axis, [(i, (i + by) % length) for i in range(length)])  54.8 us
    ppermute x8, starting transfers between devices, from_behind(): return lax.ppermute(block, axis, route)  22.4 us
    ppermute x16, starting transfers between devices, passed_along(): lax.ppermute(array, axis, [(i, (i + by) % length) for i in range(length)])  17.9 us
    add x3, other arithmetic, yee_step(): new_x = elec_x + coef * back_x + coef * amplitude * source  9.75 us
    add x3, other arithmetic, yee_step(): new_z = elec_z + coef * back_z  7.78 us
    select_n x1, other arithmetic, on_device(): eps_grad = jnp.where(material >= 2, -grad, 0.0)  4.16 us
    add x1, other arithmetic, yee_step(): new_y = elec_y + coef * back_y  2.68 us
  transfers between devices with their start and end apart: 24, of which 8 were waited for; matrix products, arithmetic and copies ran while one was open for 5% of the time, Pallas kernels for 0%

commit v1 on v0

v1 whole, which is shorter than its diff:
```python
import jax
import jax.numpy as jnp
from jax import lax
from jax.experimental import pallas as pl
from jax.experimental.pallas import tpu as pltpu
from jax.sharding import PartitionSpec as P

COURANT = 0.5
HALO = 4
BEYOND = 2
TILE = 8
GROUP = 16
WIDE = 32
TRACES = 2 * HALO
GROUPS = 1
F32 = jnp.float32


def lane_ids(shape):
    return lax.broadcasted_iota(jnp.int32, shape, 1)


def row_ids(shape):
    return lax.broadcasted_iota(jnp.int32, shape, 0)


def turn(value, shift, axis):
    shift = shift % value.shape[axis]
    if shift == 0:
        return value
    return pltpu.roll(value, shift, axis)


def x_after(value):
    return turn(value, -1, 0)


def x_before(value):
    return turn(value, 1, 0)


def swaps(size, periodic):
    first = [(i, i + 1) for i in range(0, size - 1, 2)]
    second = [(i, i + 1) for i in range(1, size - 1, 2)]
    if periodic and size > 2:
        second.append((size - 1, 0))
    both = lambda pairs: pairs + [(b, a) for a, b in pairs]
    return both(first), both(second)


def z_swaps(size, beside):
    first, second = swaps(size, False)
    wide = lambda pairs: [(a * beside + i, b * beside + i) for a, b in pairs for i in range(beside)]
    idle = [z for z in range(size) if all(z != a for a, _ in second)]
    cores = [(z * beside + i, z * beside + (i ^ 1)) for z in idle for i in range(beside)]
    return first, wide(first), second, wide(second) + cores


def pillars(depth, size):
    planes = depth * size
    return planes * 3 // 8, planes * 5 // 8


def sends_coef(depth, size, pairs):
    first, end = pillars(depth, size)
    edges = [max(a, b) * depth for a, b in pairs]
    return any(edge - BEYOND < end and edge + BEYOND > first for edge in edges)


def is_even(axis):
    return lax.rem(lax.axis_index(axis), 2) == 0


def coef_of(which, eps, count):
    permit = jnp.zeros(which.shape, F32)
    for index in range(count):
        permit = jnp.where(which == index, eps(index), permit)
    return (COURANT * COURANT) / permit


def slab_scale(c):
    return 1.0 / COURANT if 3 <= c < 6 else 1.0


def x_pack_kernel(
    fields, material, profile, eps, wave, to_a, to_b, scalars, fields_in, material_in, profile_in, eps_in, wave_in, sems
):
    depth, rows, lanes = material.shape
    pairs = ((fields, fields_in), (material, material_in), (profile, profile_in), (eps, eps_in), (wave, wave_in))
    copies = [pltpu.make_async_copy(one, two, sems.at[index]) for index, (one, two) in enumerate(pairs)]
    for copy in copies:
        copy.start()
    for copy in copies:
        copy.wait()
    even = is_even("gx")
    upper = row_ids((TILE, lanes)) < HALO

    def slab(side, s):
        c, z = divmod(s, depth)
        here = slice(0, TILE) if side == 0 else slice(rows - TILE, rows)
        if c < 6:
            return fields_in[c, z, here, :] * slab_scale(c)
        if c == 6:
            return coef_of(material_in[z, here, :], lambda index: eps_in[index], eps.shape[0])
        return profile_in[here, :]

    count = 7 * depth + 1
    for tile in range(to_a.shape[0]):
        one, two = 2 * tile, min(2 * tile + 1, count - 1)
        left = jnp.where(upper, slab(0, one), turn(slab(0, two), HALO, 0))
        right = jnp.where(upper, turn(slab(1, one), HALO, 0), slab(1, two))
        to_a[tile] = jnp.where(even, right, left)
        to_b[tile] = jnp.where(even, left, right)
    values = [wave_in[t] * (1.0 / COURANT) for t in range(HALO)] + [eps_in[i] for i in range(eps.shape[0])]
    for index, value in enumerate(values):
        scalars[index : index + 1, :] = jnp.full((1, lanes), value)


def y_pack_tile(slab, depth, lanes):
    quad = lane_ids((TILE, lanes)) // HALO
    low = jnp.zeros((TILE, lanes), F32)
    high = jnp.zeros((TILE, lanes), F32)
    for c in range(8):
        for z in range(depth):
            value = slab(c, z)
            at = WIDE * z + HALO * c
            low = jnp.where(quad == at // HALO, turn(value, at, 1), low)
            at = at + HALO
            high = jnp.where(quad == at // HALO % (lanes // HALO), turn(value, at + HALO, 1), high)
    return low, high


def y_place(out, at, low, high, both):
    here = pl.ds(at, TILE)
    if both:
        out[0, here, :], out[1, here, :] = low, high
    else:
        even = is_even("gy")
        out[0, here, :] = jnp.where(even, high, low)
        out[1, here, :] = jnp.where(even, low, high)


def x_unpack_kernel(from_a, from_b, partly, halo, out):
    depth = (halo.shape[0] - 1) // 7
    lanes = halo.shape[2]
    even = is_even("gx")
    upper = row_ids((TILE, lanes)) < HALO
    count = halo.shape[0]
    for tile in range(from_a.shape[0]):
        a, b = from_a[tile], from_b[tile]
        right = jnp.where(even, a, b)
        left = jnp.where(even, b, a)
        halo[2 * tile] = jnp.where(upper, right, turn(left, HALO, 0))
        if 2 * tile + 1 < count:
            halo[2 * tile + 1] = jnp.where(upper, turn(right, HALO, 0), left)
    slab = lambda c, z: halo[depth * c + z] if c < 7 else halo[7 * depth]
    low, high = y_pack_tile(slab, depth, lanes)
    y_place(out, out.shape[1] - TILE, low, high, lax.axis_size("gy") == 2)


def plane_amount(table, instant, z, depth):
    at = instant * (depth + 2) + z
    return table[at : at + 1, :]


def curl_of_electric(ex, ey, ez, y_ex, y_ez, z_ex, z_ey):
    curl_x = (y_ez - ez) - (z_ey - ey)
    curl_y = (z_ex - ex) - (x_after(ez) - ez)
    curl_z = (x_after(ey) - ey) - (y_ex - ex)
    return curl_x, curl_y, curl_z


def curl_of_magnetic(hx, hy, hz, y_hx, y_hz, z_hx, z_hy):
    back_x = (hz - y_hz) - (hy - z_hy)
    back_y = (hx - z_hx) - (hz - x_before(hz))
    back_z = (hy - x_before(hy)) - (hx - y_hx)
    return back_x, back_y, back_z


def alone_planes(depth, instant):
    every = list(range(depth))
    left = HALO - 1 - instant
    if left == 0:
        return [depth - 1], []
    if left == 1:
        return sorted({0, depth - 2, depth - 1} & set(every)), sorted({0, depth - 1})
    return every, every


def alone_magnetic(main, instant, depth):
    planes = alone_planes(depth, instant)[0]
    shifted = {p: (turn(main[0, p], -1, 1), turn(main[2, p], -1, 1)) for p in planes}
    for p in planes:
        ex, ey, ez = main[0, p], main[1, p], main[2, p]
        zero = jnp.zeros_like(ex)
        z_ex, z_ey = (main[0, p + 1], main[1, p + 1]) if p + 1 < depth else (zero, zero)
        curl = curl_of_electric(ex, ey, ez, *shifted[p], z_ex, z_ey)
        for c in range(2 if instant == HALO - 1 else 3):
            main[3 + c, p] = main[3 + c, p] - curl[c]


def alone_electric(main, instant, depth, coef, source):
    planes = alone_planes(depth, instant)[1]
    shifted = {p: (turn(main[3, p], 1, 1), turn(main[5, p], 1, 1)) for p in planes}
    for p in planes:
        hx, hy, hz = main[3, p], main[4, p], main[5, p]
        zero = jnp.zeros_like(hx)
        z_hx, z_hy = (main[3, p - 1], main[4, p - 1]) if p > 0 else (zero, zero)
        back = curl_of_magnetic(hx, hy, hz, *shifted[p], z_hx, z_hy)
        here = coef(p)
        main[0, p] = main[0, p] + here * (back[0] + source(p))
        main[1, p] = main[1, p] + here * back[1]
        main[2, p] = main[2, p] + here * back[2]


def interior_kernel(
    fields, material, profile, scalars, plane, coef, to_a, to_b, y_out, table, main
):
    depth, rows, lanes = material.shape
    eps = lambda index: scalars[HALO + index : HALO + index + 1, :]
    lane = lane_ids((1, lanes))
    there = plane[...] - lax.axis_index("gz") * depth
    inside = jnp.logical_and(there >= 0, there < depth)
    groups = [jnp.full((1, lanes), z, jnp.int32) for z in range(depth)]
    groups += [lane // WIDE, lane // GROUP - BEYOND]
    for instant in range(HALO):
        amount = jnp.where(inside, scalars[instant : instant + 1, :], 0.0)
        for index, group in enumerate(groups):
            at = instant * len(groups) + index
            table[at : at + 1, :] = jnp.where(group == there, amount, 0.0)
    base = HALO * len(groups)
    count = scalars.shape[0] - HALO
    table[base : base + count, :] = scalars[HALO : HALO + count, :]
    for z in range(depth):
        coef[z] = coef_of(material[z], eps, count)
        for c in range(6):
            value = fields[c, z]
            main[c, z] = value * slab_scale(c) if c >= 3 else value

    even = is_even("gz")

    def send(item, upward, downward):
        if item < to_a.shape[0]:
            to_a[item] = jnp.where(even, upward, downward)
        if item < to_b.shape[0]:
            to_b[item] = jnp.where(even, downward, upward)

    for beyond in range(BEYOND):
        send(TRACES + beyond, coef[depth - 1 - beyond], coef[beyond])
    for at in range(0, rows, TILE):
        here = pl.ds(at, TILE)

        def slab(c, z):
            if c < 6:
                return main[c, z, here, :]
            return coef[z, here, :] if c == 6 else profile[here, :]

        low, high = y_pack_tile(slab, depth, lanes)
        y_place(y_out, at, low, high, lax.axis_size("gy") == 2)
    for instant in range(HALO):
        alone_magnetic(main, instant, depth)
        for c in range(2):
            send(2 * instant + c, main[3 + c, depth - 1], main[c, 0])
        if instant < HALO - 1:
            alone_electric(
                main,
                instant,
                depth,
                lambda p: coef[p],
                lambda p: plane_amount(table, instant, p, depth) * profile[...],
            )


def own_strips_kernel(fields, coef, profile, halo, strips):
    depth, rows, lanes = coef.shape
    for at in range(0, rows + TILE, TILE):
        here = pl.ds(at, TILE)
        lane = lane_ids((TILE, lanes))
        part = lax.rem(lane, WIDE) // HALO
        on_right = jnp.logical_or(part == 1, part == 2)
        for c in range(8):
            out = jnp.zeros((TILE, lanes), F32)
            for z in range(depth):
                if at == rows:
                    value = halo[depth * c + z] if c < 7 else halo[7 * depth]
                elif c < 6:
                    value = fields[c, z, here, :] * slab_scale(c)
                else:
                    value = coef[z, here, :] if c == 6 else profile[here, :]
                first = WIDE * z + HALO
                both = jnp.where(on_right, turn(value, first + 2 * HALO, 1), turn(value, first + 4 * HALO, 1))
                out = jnp.where(lane // WIDE == z, both, out)
            strips[c, here, :] = out


def frame_kernel(
    fields, coef, profile, table, halo, own, from_one, from_two, strips, to_a, to_b, main, cells, strip
):
    depth, rows, lanes = coef.shape
    wide = rows + TILE
    shape = (wide, lanes)
    lane = lane_ids(shape)
    quad = lane // HALO
    part = lax.rem(quad, WIDE // HALO)
    if lax.axis_size("gy") == 2:
        from_right, from_left = from_one[...], from_two[...]
    else:
        even = is_even("gy")
        from_right = jnp.where(even, from_one[...], from_two[...])
        from_left = jnp.where(even, from_two[...], from_one[...])
    is_halo = jnp.logical_or(part == 3, part == 4)
    mixed = (
        jnp.where(lax.rem(quad, 2) == 0, from_right, from_left),
        jnp.where(lax.rem(quad, 2) == 0, from_left, from_right),
    )
    for c in range(8):
        value = jnp.where(is_halo, turn(mixed[c % 2], 3 * HALO - HALO * c, 1), own[c])
        strips[c] = value
        if c < 6:
            strip[c] = value
    ends = (slice(0, TILE), slice(TILE, 2 * TILE), slice(2 * TILE, 3 * TILE))
    last, first = pl.ds(rows - TILE, TILE), pl.ds(0, TILE)
    for z in range(depth):
        for c in range(6):
            main[c, z, ends[0], :] = fields[c, z, last, :] * slab_scale(c)
            main[c, z, ends[1], :] = halo[depth * c + z]
            main[c, z, ends[2], :] = fields[c, z, first, :] * slab_scale(c)
        cells[z, ends[0], :] = coef[z, last, :]
        cells[z, ends[1], :] = halo[6 * depth + z]
        cells[z, ends[2], :] = coef[z, first, :]
    cells[depth, ends[0], :] = profile[last, :]
    cells[depth, ends[1], :] = halo[7 * depth]
    cells[depth, ends[2], :] = profile[first, :]

    even = is_even("gz")
    bottom, top = lane < WIDE, lane >= WIDE * (depth - 1)
    upward = jnp.zeros(shape, F32)
    downward = jnp.zeros(shape, F32)

    for instant in range(HALO):
        alone_magnetic(main, instant, depth)
        ex, ey, ez = strip[0], strip[1], strip[2]
        z_ex = jnp.where(top, 0.0, turn(ex, -WIDE, 1))
        z_ey = jnp.where(top, 0.0, turn(ey, -WIDE, 1))
        curl = curl_of_electric(ex, ey, ez, turn(ex, -1, 1), turn(ez, -1, 1), z_ex, z_ey)
        for c in range(2 if instant == HALO - 1 else 3):
            strip[3 + c] = strip[3 + c] - curl[c]
        for c in range(2):
            item = 2 * instant + c
            here = lane // GROUP == item
            upward = jnp.where(here, turn(strip[3 + c], GROUP * item - WIDE * (depth - 1) - TILE, 1), upward)
            downward = jnp.where(here, turn(strip[c], GROUP * item - TILE, 1), downward)
            rows_at = wide + TILE * item
            ups = main[3 + c, depth - 1]
            downs = main[c, 0]
            for part_at, up_at, down_at in (
                (rows_at, TILE - instant - 1, TILE - instant),
                (rows_at + HALO, TILE + HALO + instant + 1, TILE + HALO + instant),
            ):
                up = ups[up_at : up_at + HALO, :]
                down = downs[down_at : down_at + HALO, :]
                to_a[part_at : part_at + HALO, :] = jnp.where(even, up, down)
                to_b[part_at : part_at + HALO, :] = jnp.where(even, down, up)
        if instant == HALO - 1:
            break
        alone_electric(
            main,
            instant,
            depth,
            lambda p: cells[p],
            lambda p: plane_amount(table, instant, p, depth) * cells[depth],
        )
        hx, hy, hz = strip[3], strip[4], strip[5]
        z_hx = jnp.where(bottom, 0.0, turn(hx, WIDE, 1))
        z_hy = jnp.where(bottom, 0.0, turn(hy, WIDE, 1))
        back = curl_of_magnetic(hx, hy, hz, turn(hx, 1, 1), turn(hz, 1, 1), z_hx, z_hy)
        amount = plane_amount(table, instant, depth, depth)
        strip[0] = strip[0] + strips[6] * (back[0] + amount * strips[7])
        strip[1] = strip[1] + strips[6] * back[1]
        strip[2] = strip[2] + strips[6] * back[2]
    to_a[0:wide, :] = jnp.where(even, upward, downward)
    to_b[0:wide, :] = jnp.where(even, downward, upward)
    def send(at, up, down):
        if at < to_a.shape[0]:
            to_a[at : at + TILE, :] = jnp.where(even, up, down)
        if at < to_b.shape[0]:
            to_b[at : at + TILE, :] = jnp.where(even, down, up)

    at = wide + TILE * TRACES
    for beyond in range(BEYOND):
        send(at, halo[6 * depth + depth - 1 - beyond], halo[6 * depth + beyond])
        at += TILE
    side = lanes // (BEYOND * GROUP)
    tile_lane = lane_ids((TILE, lanes))
    for begin in range(0, wide // TILE, side):
        up = jnp.zeros((TILE, lanes), F32)
        down = jnp.zeros((TILE, lanes), F32)
        for tile in range(begin, min(begin + side, wide // TILE)):
            value = strips[6, TILE * tile : TILE * (tile + 1), :]
            for beyond in range(BEYOND):
                goal = GROUP * (BEYOND * (tile - begin) + beyond)
                here = tile_lane // GROUP == goal // GROUP
                z = depth - BEYOND + beyond
                up = jnp.where(here, turn(value, goal - WIDE * z - TILE, 1), up)
                down = jnp.where(here, turn(value, goal - WIDE * beyond - TILE, 1), down)
        send(at, up, down)
        at += TILE


def received(a, b, above, here):
    even = is_even("gz")
    one, two = (a, b) if above else (b, a)
    place = lax.axis_index("gz")
    exists = place < lax.axis_size("gz") - 1 if above else place > 0
    return jnp.where(exists, jnp.where(even, one[here], two[here]), 0.0)


def coef_beyond(a, b, above, p, depth, table, shape):
    size = lax.axis_size("gz")
    first, end = pillars(depth, size)
    z = lax.axis_index("gz") * depth + p - BEYOND
    base = HALO * (depth + 2)
    quarter = COURANT * COURANT
    low, high = quarter / table[base + 1 : base + 2, :], quarter / table[base : base + 1, :]
    layer = jnp.broadcast_to(jnp.where(z < first, low, high), shape)
    one = layer if a is None else a()
    two = layer if b is None else b()
    even = is_even("gz")
    value = jnp.where(even, one, two) if above else jnp.where(even, two, one)
    return jnp.where(jnp.logical_and(z >= 0, z < depth * size), value, 0.0)


def edges_after(ex_shifted, ez, lane):
    return jnp.where(lax.rem(lane, GROUP) == HALO - 1, ex_shifted, ez)


def edges_before(hx_shifted, hz, lane):
    return jnp.where(lax.rem(lane, GROUP) == 3 * HALO, hx_shifted, hz)


def arrived_kernel(*refs):
    pass


def prepare_kernel(wide_strips, early, strips, out):
    _, wide, lanes = wide_strips.shape
    depth = lanes // WIDE
    lane = lane_ids((TILE, lanes))
    for at in range(0, wide, TILE):
        here = pl.ds(at, TILE)
        for c in range(8):
            value = wide_strips[c, here, :]
            moved = jnp.zeros((TILE, lanes), F32)
            for z in range(depth):
                goal = GROUP * (z + BEYOND)
                moved = jnp.where(lane // GROUP == z + BEYOND, turn(value, goal - WIDE * z - TILE, 1), moved)
            strips[c, here, :] = moved


def window_kernel(
    fields,
    coef,
    profile,
    halo,
    table,
    strips,
    early_a,
    early_b,
    late_a,
    late_b,
    forward,
    material,
    fields_out,
    eps_grad,
    results,
    grad,
    beside,
    sems,
):
    depth, rows, lanes = material.shape
    wide = rows + TILE
    shape = (wide, lanes)
    own = range(BEYOND, BEYOND + depth)
    first, last = own[0], own[-1]
    lane = lane_ids(shape)
    group = lane // GROUP

    late_strips = [received(late_a, late_b, above, slice(0, wide)) for above in (False, True)]
    for side, above in enumerate((False, True)):
        for item in range(TRACES):
            lost = item // 2 if above else item // 2 + 1
            beside[side, item, 0:rows, :] = received(early_a, early_b, above, item)
            at = wide + TILE * item
            right = received(late_a, late_b, above, slice(at, at + HALO))
            left = received(late_a, late_b, above, slice(at + HALO, at + TILE))
            beside[side, item, rows - lost : rows - lost + HALO, :] = right
            if lost < HALO:
                beside[side, item, rows + HALO + lost : wide, :] = left[0 : HALO - lost]
            if lost > 0:
                beside[side, item, 0:lost, :] = left[HALO - lost : HALO]
                value = beside[side, item]
                edge = turn(late_strips[side], lanes - HALO - GROUP * item, 1)
                value = jnp.where(lane >= lanes - lost, edge, value)
                lost_left = lost if above else lost - 1
                if lost_left > 0:
                    edge = turn(late_strips[side], -(GROUP * item + 3 * HALO), 1)
                    value = jnp.where(lane < lost_left, edge, value)
                beside[side, item] = value

    def trace(above, item):
        return beside[1 if above else 0, item]

    def strip_trace(above, item):
        p = last + 1 if above else first - 1
        return jnp.where(group == p, turn(late_strips[above], GROUP * (p - item), 1), 0.0)

    at = wide + TILE * TRACES
    lates = [late if late.shape[0] > at else None for late in (late_a, late_b)]
    joined = lambda top, tile: jnp.concatenate([top, tile], axis=0)
    zero = jnp.zeros(shape, F32)

    def late_tile(here, shift=0):
        return [None if late is None else (lambda late=late: turn(late[here], shift, 1)) for late in lates]

    wide_coef = {first + z: joined(coef[z], halo[6 * depth + z]) for z in range(depth)}
    for beyond in range(BEYOND):
        for above in (False, True):
            p = last + 1 + beyond if above else first - 1 - beyond
            item = TRACES + beyond
            parts = [
                None if early.shape[0] == TRACES else (lambda early=early: early[item])
                for early in (early_a, early_b)
            ]
            top = coef_beyond(*parts, above, p, depth, table, (rows, lanes))
            parts = late_tile(slice(at, at + TILE))
            wide_coef[p] = joined(top, coef_beyond(*parts, above, p, depth, table, (TILE, lanes)))
        at += TILE
    side = lanes // (BEYOND * GROUP)
    tile_group = lane_ids((TILE, lanes)) // GROUP
    tiles = []
    for tile in range(wide // TILE):
        here = slice(at + TILE * (tile // side), at + TILE * (tile // side) + TILE)
        start = BEYOND * GROUP * (tile % side)
        value = strips[6, TILE * tile : TILE * (tile + 1), :]
        low = coef_beyond(*late_tile(here, -start), False, tile_group, depth, table, (TILE, lanes))
        parts = late_tile(here, GROUP * (last + 1) - start)
        high = coef_beyond(*parts, True, tile_group, depth, table, (TILE, lanes))
        value = jnp.where(tile_group < first, low, value)
        tiles.append(jnp.where(tile_group > last, high, value))
    strip_coef = jnp.concatenate(tiles, axis=0)
    wide_profile = joined(profile[...], halo[7 * depth])
    strip = [strips[c] for c in range(6)]
    main = {}
    for c in range(6):
        for p in range(first - BEYOND, last + BEYOND + 1):
            z = p - first
            main[c, p] = joined(fields[c, z], halo[depth * c + z]) if first <= p <= last else zero
            if 3 <= c and first <= p <= last:
                main[c, p] = joined(fields[c, z] * slab_scale(c), halo[depth * c + z])
    below_factor = jnp.where(lax.axis_index("gz") > 0, 1.0, 0.0)
    strip_factor = jnp.where(group < first, below_factor, 1.0)

    copies = []

    def hand_out(source, target):
        copy = pltpu.make_async_copy(source, target, sems.at[len(copies)])
        copy.start()
        copies.append(copy)

    def magnetic_planes(instant):
        above = min(instant, HALO - 1 - instant, BEYOND - 1)
        return list(range(first - min(instant + 1, HALO - instant, BEYOND), last + above + 1))

    def electric_planes(instant):
        reach = min(instant + 1, HALO - 1 - instant, BEYOND)
        return list(range(first - reach, last + reach + 1))

    def in_groups(planes):
        size = -(-len(planes) // GROUPS)
        return [planes[at : at + size] for at in range(0, len(planes), size)]

    def rolled_after(mixed, planes):
        edge = {p: turn(mixed, -(GROUP * p + HALO), 1) for p in planes}
        ex = {p: turn(main[0, p], -1, 1) for p in planes}
        ez = {p: turn(jnp.where(lane == 0, edge[p], main[2, p]), -1, 1) for p in planes}
        return {p: (jnp.where(lane == lanes - 1, edge[p], ex[p]), ez[p]) for p in planes}

    def rolled_before(mixed, planes):
        edge = {p: turn(mixed, -(GROUP * p + 3 * HALO), 1) for p in planes}
        hx = {p: turn(main[3, p], 1, 1) for p in planes}
        hz = {p: turn(jnp.where(lane == lanes - 1, edge[p], main[5, p]), 1, 1) for p in planes}
        return {p: (jnp.where(lane == 0, edge[p], hx[p]), hz[p]) for p in planes}

    def strip_magnetic(instant):
        ex, ey, ez = strip[0:3]
        curl = curl_of_electric(ex, ey, ez, *strip_shifts)
        for c in range(3):
            strip[3 + c] = strip[3 + c] - strip_factor * curl[c]
        hx, hy, hz = strip[3:6]
        y_hx, y_hz = turn(hx, 1, 1), turn(hz, 1, 1)
        z_hx = turn(hx + strip_trace(False, 2 * instant), GROUP, 1)
        z_hy = turn(hy + strip_trace(False, 2 * instant + 1), GROUP, 1)
        return (y_hx, y_hz, z_hx, z_hy), edges_before(y_hx, hz, lane)

    def strip_shifted_electric(instant):
        ex, ey, ez = strip[0:3]
        y_ex, y_ez = turn(ex, -1, 1), turn(ez, -1, 1)
        z_ex = turn(ex + strip_trace(True, 2 * instant), -GROUP, 1)
        z_ey = turn(ey + strip_trace(True, 2 * instant + 1), -GROUP, 1)
        return (y_ex, y_ez, z_ex, z_ey), edges_after(y_ex, ez, lane)

    def strip_electric(instant):
        back = curl_of_magnetic(*strip[3:6], *strip_shifts)
        amount = plane_amount(table, instant, depth + 1, depth)
        strip[0] = strip[0] + strip_coef * (back[0] + amount * strips[7])
        strip[1] = strip[1] + strip_coef * back[1]
        strip[2] = strip[2] + strip_coef * back[2]
        return strip_shifted_electric(instant + 1)

    total = [None] * depth
    strip_shifts, mixed = strip_shifted_electric(0)
    moved = rolled_after(mixed, list(own))
    strip_shifts, mixed = strip_magnetic(0)
    for instant in range(HALO):
        item = 2 * instant
        final = instant == HALO - 1

        mixed_now = mixed
        if not final:
            strip_shifts, mixed = strip_electric(instant)
        following = electric_planes(instant)
        later = {p: (zero, zero) for p in following}
        for planes in in_groups(magnetic_planes(instant)):
            for p in planes:
                z_ex, z_ey = main[0, p + 1], main[1, p + 1]
                if p == last:
                    z_ex, z_ey = z_ex + trace(True, item), z_ey + trace(True, item + 1)
                curl = curl_of_electric(
                    main[0, p], main[1, p], main[2, p], *moved.get(p, (zero, zero)), z_ex, z_ey
                )
                for c in range(3):
                    main[3 + c, p] = main[3 + c, p] - (curl[c] if p >= first else below_factor * curl[c])
                    if final and first <= p <= last:
                        results[3 + c, p - first] = main[3 + c, p][0:rows] * COURANT
                if final and first <= p <= last:
                    z = p - first
                    hand_out(results.at[pl.ds(3, 3), z], fields_out.at[pl.ds(3, 3), z])
            later.update(rolled_before(mixed_now, [p for p in planes if p in following]))
        moved = later

        mixed_now = mixed
        if not final:
            strip_shifts, mixed = strip_magnetic(instant + 1)
        following = [] if final else magnetic_planes(instant + 1)
        later = {}
        for planes in in_groups(electric_planes(instant)):
            for p in planes:
                z_hx, z_hy = main.get((3, p - 1), zero), main.get((4, p - 1), zero)
                if p == first:
                    z_hx, z_hy = z_hx + trace(False, item), z_hy + trace(False, item + 1)
                back = curl_of_magnetic(main[3, p], main[4, p], main[5, p], *moved[p], z_hx, z_hy)
                here = wide_coef[p]
                inside = first <= p <= last
                z = p - first
                if inside:
                    push = plane_amount(table, instant, z, depth) * wide_profile
                    back = (back[0] + push, back[1], back[2])
                for c in range(3):
                    main[c, p] = main[c, p] + here * back[c]
                    if inside:
                        term = forward[instant, c, z].astype(F32) * main[c, p][0:rows]
                        total[z] = term if total[z] is None else total[z] + term
                if inside and final:
                    for c in range(3):
                        results[c, z] = main[c, p][0:rows]
                    grad[z] = jnp.where(material[z] >= 2, -total[z], 0.0)
                    hand_out(results.at[pl.ds(0, 3), z], fields_out.at[pl.ds(0, 3), z])
                    hand_out(grad.at[z], eps_grad.at[z])
            later.update(rolled_after(mixed_now, [p for p in planes if p in following]))
        moved = later
    for copy in copies:
        copy.wait()


VMEM = pl.BlockSpec(memory_space=pltpu.VMEM)
FAR = pl.BlockSpec(memory_space=pltpu.HBM)


def near(array):
    return pltpu.with_memory_space_constraint(array, pltpu.VMEM)


def far_off(array):
    return pltpu.with_memory_space_constraint(array, pltpu.HBM), FAR


def call(kernel, operands, outs, scratch=(), far=0, aliases=None, name=None, cost=None):
    specs, arrays = [], []
    for operand in operands:
        if isinstance(operand, tuple):
            specs.append(operand[1])
            arrays.append(operand[0])
        else:
            specs.append(VMEM)
            arrays.append(near(operand))
    return pl.pallas_call(
        kernel,
        out_shape=[jax.ShapeDtypeStruct(s, F32) for s in outs[:far]] + [
            pltpu.VMEM(getattr(s, "shape", s), getattr(s, "dtype", F32)) for s in outs[far:]
        ],
        in_specs=specs,
        out_specs=[FAR] * far + [VMEM] * (len(outs) - far),
        scratch_shapes=[s if not isinstance(s, tuple) else pltpu.VMEM(s, F32) for s in scratch],
        input_output_aliases=aliases or {},
        compiler_params=pltpu.CompilerParams(vmem_limit_bytes=32 * 1024 * 1024),
        cost_estimate=cost,
        name=name,
    )(*arrays)


def on_device(
    fields_in, material, material_eps, source_plane, source_wave, source_profile, forward_fields
):
    depth, rows, lanes = material.shape
    assert source_wave.shape[0] == HALO and depth * WIDE == lanes and BEYOND <= depth
    assert (depth + 2 * BEYOND) * GROUP == lanes and TRACES * GROUP == lanes
    wide = rows + TILE
    slabs = 7 * depth + 1
    tiles = (slabs + 1) // 2

    inputs = (fields_in, material, source_profile, material_eps, source_wave)
    to_a, to_b, scalars, fields_in, material, source_profile = call(
        x_pack_kernel,
        [far_off(array) for array in inputs],
        [(tiles, TILE, lanes)] * 2
        + [(HALO + material_eps.shape[0], lanes), fields_in.shape, material, source_profile.shape],
        [
            pltpu.SMEM(material_eps.shape, F32),
            pltpu.SMEM(source_wave.shape, F32),
            pltpu.SemaphoreType.DMA((5,)),
        ],
        name="x_pack",
    )
    swap_a, swap_b = swaps(lax.axis_size("gx"), True)
    from_a = lax.ppermute(to_a, "gx", swap_a)
    from_b = lax.ppermute(to_b, "gx", swap_b)

    pairs_a, z_a, pairs_b, z_b = z_swaps(lax.axis_size("gz"), lax.axis_size("gx"))
    with_coef = [sends_coef(depth, lax.axis_size("gz"), pairs) for pairs in (pairs_a, pairs_b)]
    items = [TRACES + BEYOND * sent for sent in with_coef]
    plane = jnp.broadcast_to(source_plane[None], (1, lanes))
    coef, early_a, early_b, partly, table = call(
        interior_kernel,
        [fields_in, material, source_profile, scalars, plane],
        [(depth, rows, lanes)]
        + [(count, rows, lanes) for count in items]
        + [(2, wide, lanes), (HALO * (depth + 2) + material_eps.shape[0], lanes)],
        [(6, depth, rows, lanes)],
        name="interior",
    )
    halo, y_out = call(
        x_unpack_kernel,
        [from_a, from_b, partly],
        [(slabs, TILE, lanes), (2, wide, lanes)],
        aliases={2: 1},
        name="x_unpack",
    )
    swap_a, swap_b = swaps(lax.axis_size("gy"), True)
    if lax.axis_size("gy") == 2:
        both = lax.ppermute(y_out, "gy", swap_a)
        from_one, from_two = both[0], both[1]
    else:
        from_one = lax.ppermute(y_out[0], "gy", swap_a)
        from_two = lax.ppermute(y_out[1], "gy", swap_b)

    early_a = lax.ppermute(early_a, ("gz", "gx"), z_a)
    early_b = lax.ppermute(early_b, ("gz", "gx"), z_b)
    (own,) = call(
        own_strips_kernel,
        [fields_in, coef, source_profile, halo],
        [(8, wide, lanes)],
        name="own_strips",
    )
    side = lanes // (BEYOND * GROUP)
    coef_rows = TILE * BEYOND + TILE * (-(-wide // TILE // side))
    late_rows = [wide + TILE * TRACES + coef_rows * sent for sent in with_coef]
    strips, late_a, late_b = call(
        frame_kernel,
        [fields_in, coef, source_profile, table, halo, own, from_one, from_two],
        [(8, wide, lanes)] + [(count, lanes) for count in late_rows],
        [(6, depth, 3 * TILE, lanes), (depth + 1, 3 * TILE, lanes), (6, wide, lanes)],
        name="frame",
    )
    late_a = lax.ppermute(late_a, ("gz", "gx"), z_a)
    late_b = lax.ppermute(late_b, ("gz", "gx"), z_b)

    (early_b,) = call(
        arrived_kernel,
        [early_b],
        [early_b.shape],
        aliases={0: 0},
        name="arrived",
        cost=pl.CostEstimate(flops=10**9, bytes_accessed=0, transcendentals=0),
    )
    strips, early_b = call(
        prepare_kernel,
        [strips, early_b],
        [(8, wide, lanes), early_b.shape],
        aliases={1: 1},
        name="prepare",
    )
    fields_out, eps_grad = call(
        window_kernel,
        [fields_in, coef, source_profile, halo, table, strips, early_a, early_b, late_a, late_b]
        + [forward_fields, material],
        [(6, depth, rows, lanes), (depth, rows, lanes)],
        [
            (6, depth, rows, lanes),
            (depth, rows, lanes),
            (2, TRACES, wide, lanes),
            pltpu.SemaphoreType.DMA((3 * depth,)),
        ],
        far=2,
        name="window",
    )
    return (fields_out, eps_grad)


def solution(mesh):
    placed = (
        P(None, "gz", "gx", "gy"),
        P("gz", "gx", "gy"),
        P(),
        P(),
        P(),
        P("gx", "gy"),
        P(None, None, "gz", "gx", "gy"),
    )
    return jax.shard_map(
        on_device,
        mesh=mesh,
        in_specs=placed,
        out_specs=(P(None, "gz", "gx", "gy"), P("gz", "gx", "gy")),
        check_vma=False,
    )
```

time: 133 us -> 23.4 us (0.18)
  waiting for transfers between devices: 54.8 us -> 3.36 us
  starting transfers between devices: 40.3 us -> 9.85 us
  other arithmetic: 27.2 us -> 0 us
  Pallas kernels: 0 us -> 8.65 us
  local copies, waits for them, and re-layouts: 8.2 us -> 0.01 us
    ppermute x24 -> x7, waiting for transfers between devices: 54.8 us -> 3.36 us  [the longest x1 3.03 us: on_device(): late_a = lax.ppermute(late_a, ('gz', 'gx'), z_a)]
    ppermute x24 -> x7, starting transfers between devices: 40.3 us -> 9.85 us  [the longest x1 2.86 us: on_device(): early_a = lax.ppermute(early_a, ('gz', 'gx'), z_a)]
    add x7 -> x0, other arithmetic: 20.2 us -> none  [the longest x3 9.75 us: yee_step(): new_x = elec_x + coef * back_x + coef * amplitude * source]
    pallas_call x0 -> x8, Pallas kernels: none -> 8.65 us  [call(): pl.pallas_call(kernel, out_shape=[jax.ShapeDtypeStruct(s, F32) for s in o...]
    slice x6 -> x0, local copies, waits for them, and re-layouts: 6.5 us -> none  [the longest x1 1.45 us: on_device(): permit = permit + jnp.where(material == which, material_eps[which], 0.0)]
    select_n x2 -> x0, other arithmetic: 4.16 us -> none  [the longest x1 4.16 us: on_device(): eps_grad = jnp.where(material >= 2, -grad, 0.0)]
    unnamed x15 -> x2, local copies, waits for them, and re-layouts: 1.69 us -> 0.01 us
  transfers between devices with their start and end apart: 24 -> 7, of which waited for: 8 -> 2; matrix products, arithmetic and copies ran while one was open for 5% -> 0% of each run, Pallas kernels for 0% -> 15%
where the time goes in v1:
time: 23.4 us; the launch traced here: 23.2 us
  starting transfers between devices  9.85 us (42%)
  Pallas kernels  8.65 us (37%)
  waiting for transfers between devices  3.36 us (14%)
  between operations  1.37 us (6%)
    pallas_call x8, Pallas kernels, call(): pl.pallas_call(kernel, out_shape=[jax.ShapeDtypeStruct(s, F32) for s in o...  8.65 us
    ppermute x1, waiting for transfers between devices, on_device(): late_a = lax.ppermute(late_a, ('gz', 'gx'), z_a)  3.03 us
    ppermute x1, starting transfers between devices, on_device(): early_a = lax.ppermute(early_a, ('gz', 'gx'), z_a)  2.86 us
    ppermute x1, starting transfers between devices, on_device(): from_b = lax.ppermute(to_b, 'gx', swap_b)  2.64 us
    ppermute x1, starting transfers between devices, on_device(): late_a = lax.ppermute(late_a, ('gz', 'gx'), z_a)  2.23 us
    ppermute x1, starting transfers between devices, on_device(): both = lax.ppermute(y_out, 'gy', swap_a)  1.47 us
    ppermute x1, starting transfers between devices, on_device(): from_a = lax.ppermute(to_a, 'gx', swap_a)  0.52 us
  transfers between devices with their start and end apart: 7, of which 2 were waited for; matrix products, arithmetic and copies ran while one was open for 0% of the time, Pallas kernels for 15%

profile of v1, /device:TPU:0, one launch (start us, length us, event | category | flops | bytes accessed | tf_op | source)
XLA Modules:
  0.0 23.2 jit_solution(5589943874998145795)
XLA Ops:
  0.6 1.2 %x_pack.1 = (f32[15,8,128]{2,1,0:T(8,128)S(1)}, f32[15,8,128]{2,1,0:T(8,128)S(1)}, f32[8,128]{1,0:T(8,128)S(1)}, f32[6,4,64,128]{3,2,1,0:T(8,128)S(1)}, s32[4,64...) custom-call(f32[6,4,64,128]{3,2,1,0:T(8,128)} %fields.1, s32[4,64,128]{2,1,0:T(8,128)} %material.1, f32[64,128]{1,0:T(8,128)} %profile.1, ...), custom_call_target="tpu_custom_call" | custom-call | tf_op jit(solution)/shard_map/x_pack/pallas_call | solution.py:706
  1.9 0.5 %collective-permute-start = (f32[15,8,128]{2,1,0:T(8,128)S(1)}, f32[15,8,128]{2,1,0:T(8,128)S(1)}, u32[]{:S(2)}, u32[]{:S(2)}) collective-permute-start(f32[15,8,128]{2,1,0:T(8,128)S(1)} %get-tuple-element.25), channel_id=1, source_target_pairs={{0,2},{4,6},{2,0},{6,4},{1,3},{5,7},{3,1},{7,5},{8,10},{12,14},{10... | collective-permute-start | bytes 184328 | tf_op jit(solution)/shard_map/ppermute | solution.py:745
  2.4 2.6 %collective-permute-start.1 = (f32[15,8,128]{2,1,0:T(8,128)S(1)}, f32[15,8,128]{2,1,0:T(8,128)S(1)}, u32[]{:S(2)}, u32[]{:S(2)}) collective-permute-start(f32[15,8,128]{2,1,0:T(8,128)S(1)} %get-tuple-element.26), channel_id=1, source_target_pairs={{2,4},{6,0},{4,2},{0,6},{3,5},{7,1},{5,3},{1,7},{10,12},{14,8},{12... | collective-permute-start | bytes 184328 | tf_op jit(solution)/shard_map/ppermute | solution.py:746
  5.7 1.2 %interior.1 = (f32[4,64,128]{2,1,0:T(8,128)S(1)}, f32[8,64,128]{2,1,0:T(8,128)S(1)}, f32[10,64,128]{2,1,0:T(8,128)S(1)}, f32[2,72,128]{2,1,0:T(8,128)S(1)}, f32[28,128]{1,0:T(8,128)S(1)}) custom-call(f32[6,4,64,128]{3,2,1,0:T(8,128)S(1)} %get-tuple-element.20.fields, s32[4,64,128]{2,1,0:T(8,128)S(1)} %get-tuple-element.21.material, ...), custom_call_target="tpu_custom_call" | custom-call | tf_op jit(solution)/shard_map/interior/pallas_call | solution.py:706
  6.9 0.1 collective-permute-start.3
  7.0 0.0 collective-permute-done.from_a
  7.0 0.3 %collective-permute-done.1.from_b = f32[15,8,128]{2,1,0:T(8,128)S(1)} collective-permute-done((f32[15,8,128]{2,1,0:T(8,128)S(1)}, f32[15,8,128]{2,1,0:T(8,128)S(1)}, u32[]{:S(2)}, u32[]{:S(2)}) %collective-permute-start.1) | collective-permute-done | bytes 61472 | tf_op jit(solution)/shard_map/ppermute | solution.py:746
  7.3 0.1 x_unpack.1
  7.5 1.5 %collective-permute-start.2 = (f32[2,72,128]{2,1,0:T(8,128)S(1)}, f32[2,72,128]{2,1,0:T(8,128)S(1)}, u32[]{:S(2)}, u32[]{:S(2)}) collective-permute-start(f32[2,72,128]{2,1,0:T(8,128)S(1)} %get-tuple-element.30), channel_id=1, source_target_pairs={{0,1},{1,0},{2,3},{3,2},{4,5},{5,4},{6,7},{7,6},{8,9},{9,8},{10,11... | collective-permute-start | bytes 221192 | tf_op jit(solution)/shard_map/ppermute | solution.py:770
  8.9 2.9 %collective-permute-start.4 = (f32[8,64,128]{2,1,0:T(8,128)S(1)}, f32[8,64,128]{2,1,0:T(8,128)S(1)}, u32[]{:S(2)}, u32[]{:S(2)}) collective-permute-start(f32[8,64,128]{2,1,0:T(8,128)S(1)} %get-tuple-element.34), channel_id=1, source_target_pairs={{0,8},{2,10},{4,12},{6,14},{16,24},{18,26},{20,28},{22,30},{8,0},{... | collective-permute-start | bytes 786440 | tf_op jit(solution)/shard_map/ppermute | solution.py:776
  11.8 0.7 %own_strips.1.own = f32[8,72,128]{2,1,0:T(8,128)S(1)} custom-call(f32[6,4,64,128]{3,2,1,0:T(8,128)S(1)} %get-tuple-element.20.fields, f32[4,64,128]{2,1,0:T(8,128)S(1)} %get-tuple-element.24.coef, f32[64,128]{1,0:T(8,128)S(1)} %get-tuple-element.22.profile, f32[29,8,128]{2,1,0:T(8,128)S(1)} %get-tuple-element.28.halo), custom_call_target="tpu_custom_call" | custom-call | tf_op jit(solution)/shard_map/own_strips/pallas_call | solution.py:706
  12.5 0.0 collective-permute-done.2
  12.5 1.1 %frame.1 = (f32[8,72,128]{2,1,0:T(8,128)S(1)}, f32[136,128]{1,0:T(8,128)S(1)}, f32[176,128]{1,0:T(8,128)S(1)}) custom-call(f32[6,4,64,128]{3,2,1,0:T(8,128)S(1)} %get-tuple-element.20.fields, f32[4,64,128]{2,1,0:T(8,128)S(1)} %get-tuple-element.24.coef, f32[64,128]{1,0:T(8,128)S(1)} %get-tuple-element.22.profile, f32[28,128]{1,0:T(8,128)S(1)} %get-tuple-element.29.table, ...), custom_call_target="tpu_custom_call" | custom-call | tf_op jit(solution)/shard_map/frame/pallas_call | solution.py:706
  13.6 2.2 %collective-permute-start.5 = (f32[136,128]{1,0:T(8,128)S(1)}, f32[136,128]{1,0:T(8,128)S(1)}, u32[]{:S(2)}, u32[]{:S(2)}) collective-permute-start(f32[136,128]{1,0:T(8,128)S(1)} %get-tuple-element.36), channel_id=1, source_target_pairs={{0,8},{2,10},{4,12},{6,14},{16,24},{18,26},{20,28},{22,30},{8,0},{... | collective-permute-start | bytes 208904 | tf_op jit(solution)/shard_map/ppermute | solution.py:794
  15.8 0.0 collective-permute-start.6
  15.8 0.0 collective-permute-done.3.refs_0_
  15.8 0.0 copy-start
  15.9 0.4 %prepare.1 = (f32[8,72,128]{2,1,0:T(8,128)S(1)}, f32[10,64,128]{2,1,0:T(8,128)S(1)}) custom-call(f32[8,72,128]{2,1,0:T(8,128)S(1)} %get-tuple-element.31.wide_strips, f32[10,64,128]{2,1,0:T(8,128)S(1)} %arrived.1.early), custom_call_target="tpu_custom_call", output_to_operand_aliasing={{1}: (1, {})} | custom-call | tf_op jit(solution)/shard_map/prepare/pallas_call | solution.py:706
  16.2 3.0 %collective-permute-done.5.late_a = f32[136,128]{1,0:T(8,128)S(1)} collective-permute-done((f32[136,128]{1,0:T(8,128)S(1)}, f32[136,128]{1,0:T(8,128)S(1)}, u32[]{:S(2)}, u32[]{:S(2)}) %collective-permute-start.5) | collective-permute-done | bytes 69664 | tf_op jit(solution)/shard_map/ppermute | solution.py:794
  19.3 0.0 collective-permute-done.6.late_b
  19.3 0.0 collective-permute-done.4.early_a
  19.3 0.0 copy-done
  19.3 4.0 %window.1 = (f32[6,4,64,128]{3,2,1,0:T(8,128)}, f32[4,64,128]{2,1,0:T(8,128)}) custom-call(f32[6,4,64,128]{3,2,1,0:T(8,128)S(1)} %get-tuple-element.20.fields, f32[4,64,128]{2,1,0:T(8,128)S(1)} %get-tuple-element.24.coef, f32[64,128]{1,0:T(8,128)S(1)} %get-tuple-element.22.profile, f32[29,8,128]{2,1,0:T(8,128)S(1)} %get-tuple-element.28.halo, ...), custom_call_target="tpu_custom_call" | custom-call | tf_op jit(solution)/shard_map/window/pallas_call | solution.py:706
  (3 shorter events, 0.0 us)
Async XLA Ops:
  1.9 5.1 %collective-permute-start = (f32[15,8,128]{2,1,0:T(8,128)S(1)}, f32[15,8,128]{2,1,0:T(8,128)S(1)}, u32[]{:S(2)}, u32[]{:S(2)}) collective-permute-start(f32[15,8,128]{2,1,0:T(8,128)S(1)} %get-tuple-element.25), channel_id=1, source_target_pairs={{0,2},{4,6},{2,0},{6,4},{1,3},{5,7},{3,1},{7,5},{8,10},{12,14},{10... | collective-permute-start | bytes 184328 | tf_op jit(solution)/shard_map/ppermute | solution.py:745
  2.4 4.9 %collective-permute-start.1 = (f32[15,8,128]{2,1,0:T(8,128)S(1)}, f32[15,8,128]{2,1,0:T(8,128)S(1)}, u32[]{:S(2)}, u32[]{:S(2)}) collective-permute-start(f32[15,8,128]{2,1,0:T(8,128)S(1)} %get-tuple-element.26), channel_id=1, source_target_pairs={{2,4},{6,0},{4,2},{0,6},{3,5},{7,1},{5,3},{1,7},{10,12},{14,8},{12... | collective-permute-start | bytes 184328 | tf_op jit(solution)/shard_map/ppermute | solution.py:746
  6.9 9.0 %collective-permute-start.3 = (f32[10,64,128]{2,1,0:T(8,128)S(1)}, f32[10,64,128]{2,1,0:T(8,128)S(1)}, u32[]{:S(2)}, u32[]{:S(2)}) collective-permute-start(f32[10,64,128]{2,1,0:T(8,128)S(1)} %get-tuple-element.32), channel_id=1, source_target_pairs={{8,16},{10,18},{12,20},{14,22},{16,8},{18,10},{20,12},{22,14},{0,2... | collective-permute-start | bytes 983048 | tf_op jit(solution)/shard_map/ppermute | solution.py:777
  7.5 5.0 %collective-permute-start.2 = (f32[2,72,128]{2,1,0:T(8,128)S(1)}, f32[2,72,128]{2,1,0:T(8,128)S(1)}, u32[]{:S(2)}, u32[]{:S(2)}) collective-permute-start(f32[2,72,128]{2,1,0:T(8,128)S(1)} %get-tuple-element.30), channel_id=1, source_target_pairs={{0,1},{1,0},{2,3},{3,2},{4,5},{5,4},{6,7},{7,6},{8,9},{9,8},{10,11... | collective-permute-start | bytes 221192 | tf_op jit(solution)/shard_map/ppermute | solution.py:770
  8.9 10.3 %collective-permute-start.4 = (f32[8,64,128]{2,1,0:T(8,128)S(1)}, f32[8,64,128]{2,1,0:T(8,128)S(1)}, u32[]{:S(2)}, u32[]{:S(2)}) collective-permute-start(f32[8,64,128]{2,1,0:T(8,128)S(1)} %get-tuple-element.34), channel_id=1, source_target_pairs={{0,8},{2,10},{4,12},{6,14},{16,24},{18,26},{20,28},{22,30},{8,0},{... | collective-permute-start | bytes 786440 | tf_op jit(solution)/shard_map/ppermute | solution.py:776
  13.6 5.6 %collective-permute-start.5 = (f32[136,128]{1,0:T(8,128)S(1)}, f32[136,128]{1,0:T(8,128)S(1)}, u32[]{:S(2)}, u32[]{:S(2)}) collective-permute-start(f32[136,128]{1,0:T(8,128)S(1)} %get-tuple-element.36), channel_id=1, source_target_pairs={{0,8},{2,10},{4,12},{6,14},{16,24},{18,26},{20,28},{22,30},{8,0},{... | collective-permute-start | bytes 208904 | tf_op jit(solution)/shard_map/ppermute | solution.py:794
  15.8 3.4 %collective-permute-start.6 = (f32[176,128]{1,0:T(8,128)S(1)}, f32[176,128]{1,0:T(8,128)S(1)}, u32[]{:S(2)}, u32[]{:S(2)}) collective-permute-start(f32[176,128]{1,0:T(8,128)S(1)} %get-tuple-element.37), channel_id=1, source_target_pairs={{8,16},{10,18},{12,20},{14,22},{16,8},{18,10},{20,12},{22,14},{0,2... | collective-permute-start | bytes 270344 | tf_op jit(solution)/shard_map/ppermute | solution.py:795
  15.8 3.4 %copy-start = (bf16[4,3,4,64,128]{4,3,2,1,0:T(8,128)(2,1)S(1)}, bf16[4,3,4,64,128]{4,3,2,1,0:T(8,128)(2,1)}, u32[]{:S(2)}) copy-start(bf16[4,3,4,64,128]{4,3,2,1,0:T(8,128)(2,1)} %forward.1) | copy-start | bytes 2359300

commit v2 on v1

--- a/solution.py
+++ b/solution.py
@@ -37,6 +37,15 @@
 
 def x_before(value):
     return turn(value, 1, 0)
+
+
+def early_rows(rows):
+    places, at = [], 0
+    for item in range(TRACES):
+        cut = item // 2
+        places.append((at, cut, rows - cut))
+        at += rows - 2 * cut
+    return places, at
 
 
 def swaps(size, periodic):
@@ -124,9 +133,9 @@
         for z in range(depth):
             value = slab(c, z)
             at = WIDE * z + HALO * c
-            low = jnp.where(quad == at // HALO, turn(value, at, 1), low)
-            at = at + HALO
-            high = jnp.where(quad == at // HALO % (lanes // HALO), turn(value, at + HALO, 1), high)
+            moved = turn(value, at, 1)
+            low = jnp.where(quad == at // HALO, moved, low)
+            high = jnp.where(quad == (at // HALO - 1) % (lanes // HALO), moved, high)
     return low, high
 
 
@@ -187,26 +196,28 @@
     return every, every
 
 
-def alone_magnetic(main, instant, depth):
-    planes = alone_planes(depth, instant)[0]
-    shifted = {p: (turn(main[0, p], -1, 1), turn(main[2, p], -1, 1)) for p in planes}
-    for p in planes:
+def alone_rolled(main, instant, depth, magnetic):
+    planes = alone_planes(depth, instant)[0 if magnetic else 1]
+    one, two, by = (0, 2, -1) if magnetic else (3, 5, 1)
+    return {p: (turn(main[one, p], by, 1), turn(main[two, p], by, 1)) for p in planes}
+
+
+def alone_magnetic(main, instant, depth, rolled):
+    for p in alone_planes(depth, instant)[0]:
         ex, ey, ez = main[0, p], main[1, p], main[2, p]
         zero = jnp.zeros_like(ex)
         z_ex, z_ey = (main[0, p + 1], main[1, p + 1]) if p + 1 < depth else (zero, zero)
-        curl = curl_of_electric(ex, ey, ez, *shifted[p], z_ex, z_ey)
+        curl = curl_of_electric(ex, ey, ez, *rolled[p], z_ex, z_ey)
         for c in range(2 if instant == HALO - 1 else 3):
             main[3 + c, p] = main[3 + c, p] - curl[c]
 
 
-def alone_electric(main, instant, depth, coef, source):
-    planes = alone_planes(depth, instant)[1]
-    shifted = {p: (turn(main[3, p], 1, 1), turn(main[5, p], 1, 1)) for p in planes}
-    for p in planes:
+def alone_electric(main, instant, depth, rolled, coef, source):
+    for p in alone_planes(depth, instant)[1]:
         hx, hy, hz = main[3, p], main[4, p], main[5, p]
         zero = jnp.zeros_like(hx)
         z_hx, z_hy = (main[3, p - 1], main[4, p - 1]) if p > 0 else (zero, zero)
-        back = curl_of_magnetic(hx, hy, hz, *shifted[p], z_hx, z_hy)
+        back = curl_of_magnetic(hx, hy, hz, *rolled[p], z_hx, z_hy)
         here = coef(p)
         main[0, p] = main[0, p] + here * (back[0] + source(p))
         main[1, p] = main[1, p] + here * back[1]
@@ -214,7 +225,7 @@
 
 
 def interior_kernel(
-    fields, material, profile, scalars, plane, coef, to_a, to_b, y_out, table, main
+    fields, material, profile, scalars, plane, coef, to_a, to_b, y_out, table
 ):
     depth, rows, lanes = material.shape
     eps = lambda index: scalars[HALO + index : HALO + index + 1, :]
@@ -233,39 +244,42 @@
     table[base : base + count, :] = scalars[HALO : HALO + count, :]
     for z in range(depth):
         coef[z] = coef_of(material[z], eps, count)
-        for c in range(6):
-            value = fields[c, z]
-            main[c, z] = value * slab_scale(c) if c >= 3 else value
 
     even = is_even("gz")
 
-    def send(item, upward, downward):
-        if item < to_a.shape[0]:
-            to_a[item] = jnp.where(even, upward, downward)
-        if item < to_b.shape[0]:
-            to_b[item] = jnp.where(even, downward, upward)
+    places, end = early_rows(rows)
+
+    def send(at, upward, downward):
+        here = slice(at, at + upward.shape[0])
+        if at < to_a.shape[0]:
+            to_a[here, :] = jnp.where(even, upward, downward)
+        if at < to_b.shape[0]:
+            to_b[here, :] = jnp.where(even, downward, upward)
 
     for beyond in range(BEYOND):
-        send(TRACES + beyond, coef[depth - 1 - beyond], coef[beyond])
+        send(end + rows * beyond, coef[depth - 1 - beyond], coef[beyond])
     for at in range(0, rows, TILE):
         here = pl.ds(at, TILE)
 
         def slab(c, z):
             if c < 6:
-                return main[c, z, here, :]
+                return fields[c, z, here, :] * slab_scale(c)
             return coef[z, here, :] if c == 6 else profile[here, :]
 
         low, high = y_pack_tile(slab, depth, lanes)
         y_place(y_out, at, low, high, lax.axis_size("gy") == 2)
+    main = {(c, z): fields[c, z] * slab_scale(c) for c in range(6) for z in range(depth)}
     for instant in range(HALO):
-        alone_magnetic(main, instant, depth)
+        alone_magnetic(main, instant, depth, alone_rolled(main, instant, depth, True))
         for c in range(2):
-            send(2 * instant + c, main[3 + c, depth - 1], main[c, 0])
+            at, low, high = places[2 * instant + c]
+            send(at, main[3 + c, depth - 1][low:high], main[c, 0][low:high])
         if instant < HALO - 1:
             alone_electric(
                 main,
                 instant,
                 depth,
+                alone_rolled(main, instant, depth, False),
                 lambda p: coef[p],
                 lambda p: plane_amount(table, instant, p, depth) * profile[...],
             )
@@ -294,7 +308,7 @@
 
 
 def frame_kernel(
-    fields, coef, profile, table, halo, own, from_one, from_two, strips, to_a, to_b, main, cells, strip
+    fields, coef, profile, table, halo, own, from_one, from_two, strips, to_a, to_b
 ):
     depth, rows, lanes = coef.shape
     wide = rows + TILE
@@ -308,29 +322,26 @@
         even = is_even("gy")
         from_right = jnp.where(even, from_one[...], from_two[...])
         from_left = jnp.where(even, from_two[...], from_one[...])
+    from_left = turn(from_left, 2 * HALO, 1)
     is_halo = jnp.logical_or(part == 3, part == 4)
     mixed = (
         jnp.where(lax.rem(quad, 2) == 0, from_right, from_left),
         jnp.where(lax.rem(quad, 2) == 0, from_left, from_right),
     )
+    strip = []
     for c in range(8):
         value = jnp.where(is_halo, turn(mixed[c % 2], 3 * HALO - HALO * c, 1), own[c])
         strips[c] = value
-        if c < 6:
-            strip[c] = value
-    ends = (slice(0, TILE), slice(TILE, 2 * TILE), slice(2 * TILE, 3 * TILE))
+        strip.append(value)
     last, first = pl.ds(rows - TILE, TILE), pl.ds(0, TILE)
+    around = lambda low, tile, high: jnp.concatenate([low, tile, high], axis=0)
+    main = {}
     for z in range(depth):
         for c in range(6):
-            main[c, z, ends[0], :] = fields[c, z, last, :] * slab_scale(c)
-            main[c, z, ends[1], :] = halo[depth * c + z]
-            main[c, z, ends[2], :] = fields[c, z, first, :] * slab_scale(c)
-        cells[z, ends[0], :] = coef[z, last, :]
-        cells[z, ends[1], :] = halo[6 * depth + z]
-        cells[z, ends[2], :] = coef[z, first, :]
-    cells[depth, ends[0], :] = profile[last, :]
-    cells[depth, ends[1], :] = halo[7 * depth]
-    cells[depth, ends[2], :] = profile[first, :]
+            scale = slab_scale(c)
+            main[c, z] = around(fields[c, z, last, :] * scale, halo[depth * c + z], fields[c, z, first, :] * scale)
+    cells = [around(coef[z, last, :], halo[6 * depth + z], coef[z, first, :]) for z in range(depth)]
+    cells.append(around(profile[last, :], halo[7 * depth], profile[first, :]))
 
     even = is_even("gz")
     bottom, top = lane < WIDE, lane >= WIDE * (depth - 1)
@@ -338,18 +349,17 @@
     downward = jnp.zeros(shape, F32)
 
     for instant in range(HALO):
-        alone_magnetic(main, instant, depth)
-        ex, ey, ez = strip[0], strip[1], strip[2]
+        ex, ey, ez = strip[0:3]
         z_ex = jnp.where(top, 0.0, turn(ex, -WIDE, 1))
         z_ey = jnp.where(top, 0.0, turn(ey, -WIDE, 1))
-        curl = curl_of_electric(ex, ey, ez, turn(ex, -1, 1), turn(ez, -1, 1), z_ex, z_ey)
+        y_ex, y_ez = turn(ex, -1, 1), turn(ez, -1, 1)
+        rolled = alone_rolled(main, instant, depth, True)
+        curl = curl_of_electric(ex, ey, ez, y_ex, y_ez, z_ex, z_ey)
         for c in range(2 if instant == HALO - 1 else 3):
             strip[3 + c] = strip[3 + c] - curl[c]
+        alone_magnetic(main, instant, depth, rolled)
         for c in range(2):
             item = 2 * instant + c
-            here = lane // GROUP == item
-            upward = jnp.where(here, turn(strip[3 + c], GROUP * item - WIDE * (depth - 1) - TILE, 1), upward)
-            downward = jnp.where(here, turn(strip[c], GROUP * item - TILE, 1), downward)
             rows_at = wide + TILE * item
             ups = main[3 + c, depth - 1]
             downs = main[c, 0]
@@ -361,23 +371,31 @@
                 down = downs[down_at : down_at + HALO, :]
                 to_a[part_at : part_at + HALO, :] = jnp.where(even, up, down)
                 to_b[part_at : part_at + HALO, :] = jnp.where(even, down, up)
-        if instant == HALO - 1:
-            break
-        alone_electric(
-            main,
-            instant,
-            depth,
-            lambda p: cells[p],
-            lambda p: plane_amount(table, instant, p, depth) * cells[depth],
-        )
-        hx, hy, hz = strip[3], strip[4], strip[5]
-        z_hx = jnp.where(bottom, 0.0, turn(hx, WIDE, 1))
-        z_hy = jnp.where(bottom, 0.0, turn(hy, WIDE, 1))
-        back = curl_of_magnetic(hx, hy, hz, turn(hx, 1, 1), turn(hz, 1, 1), z_hx, z_hy)
-        amount = plane_amount(table, instant, depth, depth)
-        strip[0] = strip[0] + strips[6] * (back[0] + amount * strips[7])
-        strip[1] = strip[1] + strips[6] * back[1]
-        strip[2] = strip[2] + strips[6] * back[2]
+        electric = strip[0:3]
+        if instant < HALO - 1:
+            hx, hy, hz = strip[3:6]
+            z_hx = jnp.where(bottom, 0.0, turn(hx, WIDE, 1))
+            z_hy = jnp.where(bottom, 0.0, turn(hy, WIDE, 1))
+            y_hx, y_hz = turn(hx, 1, 1), turn(hz, 1, 1)
+            rolled = alone_rolled(main, instant, depth, False)
+            back = curl_of_magnetic(hx, hy, hz, y_hx, y_hz, z_hx, z_hy)
+            amount = plane_amount(table, instant, depth, depth)
+            strip[0] = strip[0] + strip[6] * (back[0] + amount * strip[7])
+            strip[1] = strip[1] + strip[6] * back[1]
+            strip[2] = strip[2] + strip[6] * back[2]
+            alone_electric(
+                main,
+                instant,
+                depth,
+                rolled,
+                lambda p: cells[p],
+                lambda p: plane_amount(table, instant, p, depth) * cells[depth],
+            )
+        for c in range(2):
+            item = 2 * instant + c
+            here = lane // GROUP == item
+            upward = jnp.where(here, turn(strip[3 + c], GROUP * item - WIDE * (depth - 1) - TILE, 1), upward)
+            downward = jnp.where(here, turn(electric[c], GROUP * item - TILE, 1), downward)
     to_a[0:wide, :] = jnp.where(even, upward, downward)
     to_b[0:wide, :] = jnp.where(even, downward, upward)
     def send(at, up, down):
@@ -474,8 +492,8 @@
     eps_grad,
     results,
     grad,
-    beside,
     sems,
+    *beside,
 ):
     depth, rows, lanes = material.shape
     wide = rows + TILE
@@ -486,33 +504,47 @@
     group = lane // GROUP
 
     late_strips = [received(late_a, late_b, above, slice(0, wide)) for above in (False, True)]
-    for side, above in enumerate((False, True)):
-        for item in range(TRACES):
-            lost = item // 2 if above else item // 2 + 1
-            beside[side, item, 0:rows, :] = received(early_a, early_b, above, item)
-            at = wide + TILE * item
-            right = received(late_a, late_b, above, slice(at, at + HALO))
-            left = received(late_a, late_b, above, slice(at + HALO, at + TILE))
-            beside[side, item, rows - lost : rows - lost + HALO, :] = right
-            if lost < HALO:
-                beside[side, item, rows + HALO + lost : wide, :] = left[0 : HALO - lost]
-            if lost > 0:
-                beside[side, item, 0:lost, :] = left[HALO - lost : HALO]
-                value = beside[side, item]
-                edge = turn(late_strips[side], lanes - HALO - GROUP * item, 1)
-                value = jnp.where(lane >= lanes - lost, edge, value)
-                lost_left = lost if above else lost - 1
-                if lost_left > 0:
-                    edge = turn(late_strips[side], -(GROUP * item + 3 * HALO), 1)
-                    value = jnp.where(lane < lost_left, edge, value)
-                beside[side, item] = value
+    places, early_end = early_rows(rows)
+    traces = {}
+
+    def merge(above, item):
+        lost = item // 2 if above else item // 2 + 1
+        whole = beside[TRACES * above + item]
+        at, low, high = places[item]
+        whole[low:high, :] = received(early_a, early_b, above, slice(at, at + high - low))
+        at = wide + TILE * item
+        right = received(late_a, late_b, above, slice(at, at + HALO))
+        left = received(late_a, late_b, above, slice(at + HALO, at + TILE))
+        whole[rows - lost : rows - lost + HALO, :] = right
+        if lost < HALO:
+            whole[rows + HALO + lost : wide, :] = left[0 : HALO - lost]
+        if lost > 0:
+            whole[0:lost, :] = left[HALO - lost : HALO]
+        value = whole[...]
+        if lost > 0:
+            edge = turn(late_strips[above], lanes - HALO - GROUP * item, 1)
+            value = jnp.where(lane >= lanes - lost, edge, value)
+        lost_left = lost if above else lost - 1
+        if lost_left > 0:
+            edge = turn(late_strips[above], -(GROUP * item + 3 * HALO), 1)
+            value = jnp.where(lane < lost_left, edge, value)
+        traces[above, item] = value
 
     def trace(above, item):
-        return beside[1 if above else 0, item]
-
-    def strip_trace(above, item):
-        p = last + 1 if above else first - 1
-        return jnp.where(group == p, turn(late_strips[above], GROUP * (p - item), 1), 0.0)
+        return traces[above, item]
+
+    def strip_neighbours(above, item, one, two):
+        goal = last if above else first - 1
+        moved = turn(late_strips[above], GROUP * (goal - item), 1)
+        at_goal, at_next = group == goal, group == goal + 1
+        by = -GROUP if above else GROUP
+        if above:
+            one = turn(one, by, 1)
+            two = turn(jnp.where(at_next, two + moved, two), by, 1)
+            return jnp.where(at_goal, one + moved, one), two
+        one = turn(jnp.where(at_goal, one + moved, one), by, 1)
+        two = turn(two, by, 1)
+        return one, jnp.where(at_next, two + moved, two)
 
     at = wide + TILE * TRACES
     lates = [late if late.shape[0] > at else None for late in (late_a, late_b)]
@@ -526,9 +558,9 @@
     for beyond in range(BEYOND):
         for above in (False, True):
             p = last + 1 + beyond if above else first - 1 - beyond
-            item = TRACES + beyond
+            from_early = slice(early_end + rows * beyond, early_end + rows * (beyond + 1))
             parts = [
-                None if early.shape[0] == TRACES else (lambda early=early: early[item])
+                None if early.shape[0] == early_end else (lambda early=early: early[from_early])
                 for early in (early_a, early_b)
             ]
             top = coef_beyond(*parts, above, p, depth, table, (rows, lanes))
@@ -598,15 +630,13 @@
             strip[3 + c] = strip[3 + c] - strip_factor * curl[c]
         hx, hy, hz = strip[3:6]
         y_hx, y_hz = turn(hx, 1, 1), turn(hz, 1, 1)
-        z_hx = turn(hx + strip_trace(False, 2 * instant), GROUP, 1)
-        z_hy = turn(hy + strip_trace(False, 2 * instant + 1), GROUP, 1)
+        z_hx, z_hy = strip_neighbours(False, 2 * instant, hx, hy)
         return (y_hx, y_hz, z_hx, z_hy), edges_before(y_hx, hz, lane)
 
     def strip_shifted_electric(instant):
         ex, ey, ez = strip[0:3]
         y_ex, y_ez = turn(ex, -1, 1), turn(ez, -1, 1)
-        z_ex = turn(ex + strip_trace(True, 2 * instant), -GROUP, 1)
-        z_ey = turn(ey + strip_trace(True, 2 * instant + 1), -GROUP, 1)
+        z_ex, z_ey = strip_neighbours(True, 2 * instant, ex, ey)
         return (y_ex, y_ez, z_ex, z_ey), edges_after(y_ex, ez, lane)
 
     def strip_electric(instant):
@@ -618,6 +648,8 @@
         return strip_shifted_electric(instant + 1)
 
     total = [None] * depth
+    merge(True, 0)
+    merge(True, 1)
     strip_shifts, mixed = strip_shifted_electric(0)
     moved = rolled_after(mixed, list(own))
     strip_shifts, mixed = strip_magnetic(0)
@@ -628,6 +660,8 @@
         mixed_now = mixed
         if not final:
             strip_shifts, mixed = strip_electric(instant)
+        merge(False, item)
+        merge(False, item + 1)
         following = electric_planes(instant)
         later = {p: (zero, zero) for p in following}
         for planes in in_groups(magnetic_planes(instant)):
@@ -651,6 +685,8 @@
         mixed_now = mixed
         if not final:
             strip_shifts, mixed = strip_magnetic(instant + 1)
+            merge(True, item + 2)
+            merge(True, item + 3)
         following = [] if final else magnetic_planes(instant + 1)
         later = {}
         for planes in in_groups(electric_planes(instant)):
@@ -747,15 +783,14 @@
 
     pairs_a, z_a, pairs_b, z_b = z_swaps(lax.axis_size("gz"), lax.axis_size("gx"))
     with_coef = [sends_coef(depth, lax.axis_size("gz"), pairs) for pairs in (pairs_a, pairs_b)]
-    items = [TRACES + BEYOND * sent for sent in with_coef]
+    early_counts = [early_rows(rows)[1] + rows * BEYOND * sent for sent in with_coef]
     plane = jnp.broadcast_to(source_plane[None], (1, lanes))
     coef, early_a, early_b, partly, table = call(
         interior_kernel,
         [fields_in, material, source_profile, scalars, plane],
         [(depth, rows, lanes)]
-        + [(count, rows, lanes) for count in items]
+        + [(count, lanes) for count in early_counts]
         + [(2, wide, lanes), (HALO * (depth + 2) + material_eps.shape[0], lanes)],
-        [(6, depth, rows, lanes)],
         name="interior",
     )
     halo, y_out = call(
@@ -788,7 +823,6 @@
         frame_kernel,
         [fields_in, coef, source_profile, table, halo, own, from_one, from_two],
         [(8, wide, lanes)] + [(count, lanes) for count in late_rows],
-        [(6, depth, 3 * TILE, lanes), (depth + 1, 3 * TILE, lanes), (6, wide, lanes)],
         name="frame",
     )
     late_a = lax.ppermute(late_a, ("gz", "gx"), z_a)
@@ -817,9 +851,9 @@
         [
             (6, depth, rows, lanes),
             (depth, rows, lanes),
-            (2, TRACES, wide, lanes),
             pltpu.SemaphoreType.DMA((3 * depth,)),
-        ],
+        ]
+        + [(wide, lanes)] * (2 * TRACES),
         far=2,
         name="window",
     )

time: 23.4 us -> 22.6 us (0.966)
  Pallas kernels: 8.65 us -> 7.95 us
  starting transfers between devices: 9.85 us -> 9.57 us
    pallas_call x8, Pallas kernels: 8.65 us -> 7.95 us  [call(): pl.pallas_call(kernel, out_shape=[jax.ShapeDtypeStruct(s, F32) for s in o...]
    ppermute x1, waiting for transfers between devices: 0.32 us -> 0.6 us  [on_device(): from_b = lax.ppermute(to_b, 'gx', swap_b)]
    ppermute x1, starting transfers between devices: 2.86 us -> 2.58 us  [on_device(): early_a = lax.ppermute(early_a, ('gz', 'gx'), z_a)]
  transfers between devices with their start and end apart: 7 -> 7, of which waited for: 2 -> 2; matrix products, arithmetic and copies ran while one was open for 0% -> 0% of each run, Pallas kernels for 15% -> 13%
where the time goes in v2:
time: 22.6 us; the launch traced here: 22.4 us
  starting transfers between devices  9.57 us (42%)
  Pallas kernels  7.95 us (35%)
  waiting for transfers between devices  3.51 us (16%)
  between operations  1.37 us (6%)
    pallas_call x8, Pallas kernels, call(): pl.pallas_call(kernel, out_shape=[jax.ShapeDtypeStruct(s, F32) for s in o...  7.95 us
    ppermute x1, waiting for transfers between devices, on_device(): late_a = lax.ppermute(late_a, ('gz', 'gx'), z_a)  2.89 us
    ppermute x1, starting transfers between devices, on_device(): from_b = lax.ppermute(to_b, 'gx', swap_b)  2.64 us
    ppermute x1, starting transfers between devices, on_device(): early_a = lax.ppermute(early_a, ('gz', 'gx'), z_a)  2.58 us
    ppermute x1, starting transfers between devices, on_device(): late_a = lax.ppermute(late_a, ('gz', 'gx'), z_a)  2.23 us
    ppermute x1, starting transfers between devices, on_device(): both = lax.ppermute(y_out, 'gy', swap_a)  1.47 us
    ppermute x1, waiting for transfers between devices, on_device(): from_b = lax.ppermute(to_b, 'gx', swap_b)  0.6 us
    ppermute x1, starting transfers between devices, on_device(): from_a = lax.ppermute(to_a, 'gx', swap_a)  0.52 us
  transfers between devices with their start and end apart: 7, of which 2 were waited for; matrix products, arithmetic and copies ran while one was open for 0% of the time, Pallas kernels for 13%

profile of v2, /device:TPU:0, one launch (start us, length us, event | category | flops | bytes accessed | tf_op | source)
XLA Modules:
  0.0 22.4 jit_solution(11907950961426969851)
XLA Ops:
  0.6 1.2 %x_pack.1 = (f32[15,8,128]{2,1,0:T(8,128)S(1)}, f32[15,8,128]{2,1,0:T(8,128)S(1)}, f32[8,128]{1,0:T(8,128)S(1)}, f32[6,4,64,128]{3,2,1,0:T(8,128)S(1)}, s32[4,64...) custom-call(f32[6,4,64,128]{3,2,1,0:T(8,128)} %fields.1, s32[4,64,128]{2,1,0:T(8,128)} %material.1, f32[64,128]{1,0:T(8,128)} %profile.1, ...), custom_call_target="tpu_custom_call" | custom-call | tf_op jit(solution)/shard_map/x_pack/pallas_call | solution.py:742
  1.9 0.5 %collective-permute-start = (f32[15,8,128]{2,1,0:T(8,128)S(1)}, f32[15,8,128]{2,1,0:T(8,128)S(1)}, u32[]{:S(2)}, u32[]{:S(2)}) collective-permute-start(f32[15,8,128]{2,1,0:T(8,128)S(1)} %get-tuple-element.25), channel_id=1, source_target_pairs={{0,2},{4,6},{2,0},{6,4},{1,3},{5,7},{3,1},{7,5},{8,10},{12,14},{10... | collective-permute-start | bytes 184328 | tf_op jit(solution)/shard_map/ppermute | solution.py:781
  2.4 2.6 %collective-permute-start.1 = (f32[15,8,128]{2,1,0:T(8,128)S(1)}, f32[15,8,128]{2,1,0:T(8,128)S(1)}, u32[]{:S(2)}, u32[]{:S(2)}) collective-permute-start(f32[15,8,128]{2,1,0:T(8,128)S(1)} %get-tuple-element.26), channel_id=1, source_target_pairs={{2,4},{6,0},{4,2},{0,6},{3,5},{7,1},{5,3},{1,7},{10,12},{14,8},{12... | collective-permute-start | bytes 184328 | tf_op jit(solution)/shard_map/ppermute | solution.py:782
  5.7 0.9 %interior.1 = (f32[4,64,128]{2,1,0:T(8,128)S(1)}, f32[488,128]{1,0:T(8,128)S(1)}, f32[616,128]{1,0:T(8,128)S(1)}, f32[2,72,128]{2,1,0:T(8,128)S(1)}, f32[28,128]{1,0:T(8,128)S(1)}) custom-call(f32[6,4,64,128]{3,2,1,0:T(8,128)S(1)} %get-tuple-element.20.fields, s32[4,64,128]{2,1,0:T(8,128)S(1)} %get-tuple-element.21.material, ...), custom_call_target="tpu_custom_call" | custom-call | tf_op jit(solution)/shard_map/interior/pallas_call | solution.py:742
  6.6 0.1 collective-permute-start.3
  6.7 0.0 collective-permute-done.from_a
  6.7 0.6 %collective-permute-done.1.from_b = f32[15,8,128]{2,1,0:T(8,128)S(1)} collective-permute-done((f32[15,8,128]{2,1,0:T(8,128)S(1)}, f32[15,8,128]{2,1,0:T(8,128)S(1)}, u32[]{:S(2)}, u32[]{:S(2)}) %collective-permute-start.1) | collective-permute-done | bytes 61472 | tf_op jit(solution)/shard_map/ppermute | solution.py:782
  7.3 0.1 x_unpack.1
  7.4 1.5 %collective-permute-start.2 = (f32[2,72,128]{2,1,0:T(8,128)S(1)}, f32[2,72,128]{2,1,0:T(8,128)S(1)}, u32[]{:S(2)}, u32[]{:S(2)}) collective-permute-start(f32[2,72,128]{2,1,0:T(8,128)S(1)} %get-tuple-element.30), channel_id=1, source_target_pairs={{0,1},{1,0},{2,3},{3,2},{4,5},{5,4},{6,7},{7,6},{8,9},{9,8},{10,11... | collective-permute-start | bytes 221192 | tf_op jit(solution)/shard_map/ppermute | solution.py:805
  8.9 2.6 %collective-permute-start.4 = (f32[488,128]{1,0:T(8,128)S(1)}, f32[488,128]{1,0:T(8,128)S(1)}, u32[]{:S(2)}, u32[]{:S(2)}) collective-permute-start(f32[488,128]{1,0:T(8,128)S(1)} %get-tuple-element.34), channel_id=1, source_target_pairs={{0,8},{2,10},{4,12},{6,14},{16,24},{18,26},{20,28},{22,30},{8,0},{... | collective-permute-start | bytes 749576 | tf_op jit(solution)/shard_map/ppermute | solution.py:811
  11.5 0.7 %own_strips.1.own = f32[8,72,128]{2,1,0:T(8,128)S(1)} custom-call(f32[6,4,64,128]{3,2,1,0:T(8,128)S(1)} %get-tuple-element.20.fields, f32[4,64,128]{2,1,0:T(8,128)S(1)} %get-tuple-element.24.coef, f32[64,128]{1,0:T(8,128)S(1)} %get-tuple-element.22.profile, f32[29,8,128]{2,1,0:T(8,128)S(1)} %get-tuple-element.28.halo), custom_call_target="tpu_custom_call" | custom-call | tf_op jit(solution)/shard_map/own_strips/pallas_call | solution.py:742
  12.2 0.0 collective-permute-done.2
  12.2 1.0 %frame.1 = (f32[8,72,128]{2,1,0:T(8,128)S(1)}, f32[136,128]{1,0:T(8,128)S(1)}, f32[176,128]{1,0:T(8,128)S(1)}) custom-call(f32[6,4,64,128]{3,2,1,0:T(8,128)S(1)} %get-tuple-element.20.fields, f32[4,64,128]{2,1,0:T(8,128)S(1)} %get-tuple-element.24.coef, f32[64,128]{1,0:T(8,128)S(1)} %get-tuple-element.22.profile, f32[28,128]{1,0:T(8,128)S(1)} %get-tuple-element.29.table, ...), custom_call_target="tpu_custom_call" | custom-call | tf_op jit(solution)/shard_map/frame/pallas_call | solution.py:742
  13.2 2.2 %collective-permute-start.5 = (f32[136,128]{1,0:T(8,128)S(1)}, f32[136,128]{1,0:T(8,128)S(1)}, u32[]{:S(2)}, u32[]{:S(2)}) collective-permute-start(f32[136,128]{1,0:T(8,128)S(1)} %get-tuple-element.36), channel_id=1, source_target_pairs={{0,8},{2,10},{4,12},{6,14},{16,24},{18,26},{20,28},{22,30},{8,0},{... | collective-permute-start | bytes 208904 | tf_op jit(solution)/shard_map/ppermute | solution.py:828
  15.4 0.0 collective-permute-start.6
  15.4 0.0 collective-permute-done.3.refs_0_
  15.4 0.0 copy-start
  15.4 0.4 %prepare.1 = (f32[8,72,128]{2,1,0:T(8,128)S(1)}, f32[616,128]{1,0:T(8,128)S(1)}) custom-call(f32[8,72,128]{2,1,0:T(8,128)S(1)} %get-tuple-element.31.wide_strips, f32[616,128]{1,0:T(8,128)S(1)} %arrived.1.early), custom_call_target="tpu_custom_call", output_to_operand_aliasing={{1}: (1, {})} | custom-call | tf_op jit(solution)/shard_map/prepare/pallas_call | solution.py:742
  15.8 2.9 %collective-permute-done.5.late_a = f32[136,128]{1,0:T(8,128)S(1)} collective-permute-done((f32[136,128]{1,0:T(8,128)S(1)}, f32[136,128]{1,0:T(8,128)S(1)}, u32[]{:S(2)}, u32[]{:S(2)}) %collective-permute-start.5) | collective-permute-done | bytes 69664 | tf_op jit(solution)/shard_map/ppermute | solution.py:828
  18.7 0.0 collective-permute-done.6.late_b
  18.7 0.0 collective-permute-done.4.early_a
  18.7 0.0 copy-done
  18.7 3.7 %window.1 = (f32[6,4,64,128]{3,2,1,0:T(8,128)}, f32[4,64,128]{2,1,0:T(8,128)}) custom-call(f32[6,4,64,128]{3,2,1,0:T(8,128)S(1)} %get-tuple-element.20.fields, f32[4,64,128]{2,1,0:T(8,128)S(1)} %get-tuple-element.24.coef, f32[64,128]{1,0:T(8,128)S(1)} %get-tuple-element.22.profile, f32[29,8,128]{2,1,0:T(8,128)S(1)} %get-tuple-element.28.halo, ...), custom_call_target="tpu_custom_call" | custom-call | tf_op jit(solution)/shard_map/window/pallas_call | solution.py:742
  (3 shorter events, 0.0 us)
Async XLA Ops:
  1.9 4.8 %collective-permute-start = (f32[15,8,128]{2,1,0:T(8,128)S(1)}, f32[15,8,128]{2,1,0:T(8,128)S(1)}, u32[]{:S(2)}, u32[]{:S(2)}) collective-permute-start(f32[15,8,128]{2,1,0:T(8,128)S(1)} %get-tuple-element.25), channel_id=1, source_target_pairs={{0,2},{4,6},{2,0},{6,4},{1,3},{5,7},{3,1},{7,5},{8,10},{12,14},{10... | collective-permute-start | bytes 184328 | tf_op jit(solution)/shard_map/ppermute | solution.py:781
  2.4 4.9 %collective-permute-start.1 = (f32[15,8,128]{2,1,0:T(8,128)S(1)}, f32[15,8,128]{2,1,0:T(8,128)S(1)}, u32[]{:S(2)}, u32[]{:S(2)}) collective-permute-start(f32[15,8,128]{2,1,0:T(8,128)S(1)} %get-tuple-element.26), channel_id=1, source_target_pairs={{2,4},{6,0},{4,2},{0,6},{3,5},{7,1},{5,3},{1,7},{10,12},{14,8},{12... | collective-permute-start | bytes 184328 | tf_op jit(solution)/shard_map/ppermute | solution.py:782
  6.6 8.8 %collective-permute-start.3 = (f32[616,128]{1,0:T(8,128)S(1)}, f32[616,128]{1,0:T(8,128)S(1)}, u32[]{:S(2)}, u32[]{:S(2)}) collective-permute-start(f32[616,128]{1,0:T(8,128)S(1)} %get-tuple-element.32), channel_id=1, source_target_pairs={{8,16},{10,18},{12,20},{14,22},{16,8},{18,10},{20,12},{22,14},{0,2... | collective-permute-start | bytes 946184 | tf_op jit(solution)/shard_map/ppermute | solution.py:812
  7.4 4.7 %collective-permute-start.2 = (f32[2,72,128]{2,1,0:T(8,128)S(1)}, f32[2,72,128]{2,1,0:T(8,128)S(1)}, u32[]{:S(2)}, u32[]{:S(2)}) collective-permute-start(f32[2,72,128]{2,1,0:T(8,128)S(1)} %get-tuple-element.30), channel_id=1, source_target_pairs={{0,1},{1,0},{2,3},{3,2},{4,5},{5,4},{6,7},{7,6},{8,9},{9,8},{10,11... | collective-permute-start | bytes 221192 | tf_op jit(solution)/shard_map/ppermute | solution.py:805
  8.9 9.8 %collective-permute-start.4 = (f32[488,128]{1,0:T(8,128)S(1)}, f32[488,128]{1,0:T(8,128)S(1)}, u32[]{:S(2)}, u32[]{:S(2)}) collective-permute-start(f32[488,128]{1,0:T(8,128)S(1)} %get-tuple-element.34), channel_id=1, source_target_pairs={{0,8},{2,10},{4,12},{6,14},{16,24},{18,26},{20,28},{22,30},{8,0},{... | collective-permute-start | bytes 749576 | tf_op jit(solution)/shard_map/ppermute | solution.py:811
  13.2 5.5 %collective-permute-start.5 = (f32[136,128]{1,0:T(8,128)S(1)}, f32[136,128]{1,0:T(8,128)S(1)}, u32[]{:S(2)}, u32[]{:S(2)}) collective-permute-start(f32[136,128]{1,0:T(8,128)S(1)} %get-tuple-element.36), channel_id=1, source_target_pairs={{0,8},{2,10},{4,12},{6,14},{16,24},{18,26},{20,28},{22,30},{8,0},{... | collective-permute-start | bytes 208904 | tf_op jit(solution)/shard_map/ppermute | solution.py:828
  15.4 3.3 %collective-permute-start.6 = (f32[176,128]{1,0:T(8,128)S(1)}, f32[176,128]{1,0:T(8,128)S(1)}, u32[]{:S(2)}, u32[]{:S(2)}) collective-permute-start(f32[176,128]{1,0:T(8,128)S(1)} %get-tuple-element.37), channel_id=1, source_target_pairs={{8,16},{10,18},{12,20},{14,22},{16,8},{18,10},{20,12},{22,14},{0,2... | collective-permute-start | bytes 270344 | tf_op jit(solution)/shard_map/ppermute | solution.py:829
  15.4 3.3 %copy-start = (bf16[4,3,4,64,128]{4,3,2,1,0:T(8,128)(2,1)S(1)}, bf16[4,3,4,64,128]{4,3,2,1,0:T(8,128)(2,1)}, u32[]{:S(2)}) copy-start(bf16[4,3,4,64,128]{4,3,2,1,0:T(8,128)(2,1)} %forward.1) | copy-start | bytes 2359300

commit v3 on v2

--- a/solution.py
+++ b/solution.py
@@ -92,10 +92,11 @@
 
 
 def x_pack_kernel(
-    fields, material, profile, eps, wave, to_a, to_b, scalars, fields_in, material_in, profile_in, eps_in, wave_in, sems
+    fields, material, profile, eps, wave, to_a, to_b, scalars, material_in, profile_in, face, eps_in, wave_in, sems
 ):
     depth, rows, lanes = material.shape
-    pairs = ((fields, fields_in), (material, material_in), (profile, profile_in), (eps, eps_in), (wave, wave_in))
+    pairs = [(material, material_in), (profile, profile_in), (eps, eps_in), (wave, wave_in)]
+    pairs = [(fields.at[:, :, pl.ds(at, TILE), :], face.at[i]) for i, at in enumerate((0, rows - TILE))] + pairs
     copies = [pltpu.make_async_copy(one, two, sems.at[index]) for index, (one, two) in enumerate(pairs)]
     for copy in copies:
         copy.start()
@@ -108,7 +109,7 @@
         c, z = divmod(s, depth)
         here = slice(0, TILE) if side == 0 else slice(rows - TILE, rows)
         if c < 6:
-            return fields_in[c, z, here, :] * slab_scale(c)
+            return face[side, c, z] * slab_scale(c)
         if c == 6:
             return coef_of(material_in[z, here, :], lambda index: eps_in[index], eps.shape[0])
         return profile_in[here, :]
@@ -460,9 +461,37 @@
     pass
 
 
-def prepare_kernel(wide_strips, early, strips, out):
+def rolled_after(main, mixed, planes, lane):
+    end = lane.shape[1] - 1
+    edge = {p: turn(mixed, -(GROUP * p + HALO), 1) for p in planes}
+    ex = {p: turn(main[0, p], -1, 1) for p in planes}
+    ez = {p: turn(jnp.where(lane == 0, edge[p], main[2, p]), -1, 1) for p in planes}
+    return {p: (jnp.where(lane == end, edge[p], ex[p]), ez[p]) for p in planes}
+
+
+def rolled_before(main, mixed, planes, lane):
+    end = lane.shape[1] - 1
+    edge = {p: turn(mixed, -(GROUP * p + 3 * HALO), 1) for p in planes}
+    hx = {p: turn(main[3, p], 1, 1) for p in planes}
+    hz = {p: turn(jnp.where(lane == end, edge[p], main[5, p]), 1, 1) for p in planes}
+    return {p: (jnp.where(lane == 0, edge[p], hx[p]), hz[p]) for p in planes}
+
+
+def below_factors(group):
+    factor = jnp.where(lax.axis_index("gz") > 0, 1.0, 0.0)
+    return factor, jnp.where(group < BEYOND, factor, 1.0)
+
+
+def wide_field(fields, halo, c, z):
+    depth = fields.shape[1]
+    own = fields[c, z] * slab_scale(c) if c >= 3 else fields[c, z]
+    return jnp.concatenate([own, halo[depth * c + z]], axis=0)
+
+
+def prepare_kernel(fields, halo, wide_strips, early, strips, magnetic, shifted, out):
     _, wide, lanes = wide_strips.shape
     depth = lanes // WIDE
+    first, last = BEYOND, BEYOND + depth - 1
     lane = lane_ids((TILE, lanes))
     for at in range(0, wide, TILE):
         here = pl.ds(at, TILE)
@@ -473,6 +502,30 @@
                 goal = GROUP * (z + BEYOND)
                 moved = jnp.where(lane // GROUP == z + BEYOND, turn(value, goal - WIDE * z - TILE, 1), moved)
             strips[c, here, :] = moved
+    lane = lane_ids((wide, lanes))
+    below_factor, strip_factor = below_factors(lane // GROUP)
+    ex, ey, ez, hx, hy, hz = [strips[c] for c in range(6)]
+    y_ex, y_ez = turn(ex, -1, 1), turn(ez, -1, 1)
+    curl = curl_of_electric(ex, ey, ez, y_ex, y_ez, turn(ex, -GROUP, 1), turn(ey, -GROUP, 1))
+    hx, hy, hz = [value - strip_factor * curl[c] for c, value in enumerate((hx, hy, hz))]
+    for c, value in enumerate((hx, hy, hz)):
+        magnetic[c, depth + 1] = value
+    zero = jnp.zeros((wide, lanes), F32)
+    main = {(c, first + z): wide_field(fields, halo, c, z) for c in range(6) for z in range(depth)}
+    for c in range(6):
+        main[c, first - 1] = main[c, last + 1] = zero
+    moved = rolled_after(main, edges_after(y_ex, ez, lane), range(first, last + 1), lane)
+    mixed = edges_before(turn(hx, 1, 1), hz, lane)
+    for p in range(first - 1, last + 1):
+        curl = curl_of_electric(
+            main[0, p], main[1, p], main[2, p], *moved.get(p, (zero, zero)), main[0, p + 1], main[1, p + 1]
+        )
+        for c in range(3):
+            main[3 + c, p] = main[3 + c, p] - (curl[c] if p >= first else below_factor * curl[c])
+            magnetic[c, p - first + 1] = main[3 + c, p]
+    moved = rolled_before(main, mixed, range(first - 1, last), lane)
+    for p in range(first - 1, last):
+        shifted[0, p - first + 1], shifted[1, p - first + 1] = moved[p]
 
 
 def window_kernel(
@@ -482,6 +535,8 @@
     halo,
     table,
     strips,
+    magnetic,
+    shifted,
     early_a,
     early_b,
     late_a,
@@ -582,15 +637,14 @@
     strip_coef = jnp.concatenate(tiles, axis=0)
     wide_profile = joined(profile[...], halo[7 * depth])
     strip = [strips[c] for c in range(6)]
-    main = {}
-    for c in range(6):
-        for p in range(first - BEYOND, last + BEYOND + 1):
-            z = p - first
-            main[c, p] = joined(fields[c, z], halo[depth * c + z]) if first <= p <= last else zero
-            if 3 <= c and first <= p <= last:
-                main[c, p] = joined(fields[c, z] * slab_scale(c), halo[depth * c + z])
-    below_factor = jnp.where(lax.axis_index("gz") > 0, 1.0, 0.0)
-    strip_factor = jnp.where(group < first, below_factor, 1.0)
+    main = {(c, p): zero for c in range(6) for p in range(first - BEYOND, last + BEYOND + 1)}
+    for c in range(3):
+        for z in range(depth):
+            main[c, first + z] = wide_field(fields, halo, c, z)
+        for p in range(first - 1, last + 1):
+            main[3 + c, p] = magnetic[c, p - first + 1]
+        strip[3 + c] = magnetic[c, depth + 1]
+    below_factor, strip_factor = below_factors(group)
 
     copies = []
 
@@ -610,24 +664,15 @@
     def in_groups(planes):
         size = -(-len(planes) // GROUPS)
         return [planes[at : at + size] for at in range(0, len(planes), size)]
-
-    def rolled_after(mixed, planes):
-        edge = {p: turn(mixed, -(GROUP * p + HALO), 1) for p in planes}
-        ex = {p: turn(main[0, p], -1, 1) for p in planes}
-        ez = {p: turn(jnp.where(lane == 0, edge[p], main[2, p]), -1, 1) for p in planes}
-        return {p: (jnp.where(lane == lanes - 1, edge[p], ex[p]), ez[p]) for p in planes}
-
-    def rolled_before(mixed, planes):
-        edge = {p: turn(mixed, -(GROUP * p + 3 * HALO), 1) for p in planes}
-        hx = {p: turn(main[3, p], 1, 1) for p in planes}
-        hz = {p: turn(jnp.where(lane == lanes - 1, edge[p], main[5, p]), 1, 1) for p in planes}
-        return {p: (jnp.where(lane == 0, edge[p], hx[p]), hz[p]) for p in planes}
 
     def strip_magnetic(instant):
         ex, ey, ez = strip[0:3]
         curl = curl_of_electric(ex, ey, ez, *strip_shifts)
         for c in range(3):
             strip[3 + c] = strip[3 + c] - strip_factor * curl[c]
+        return strip_shifted_magnetic(instant)
+
+    def strip_shifted_magnetic(instant):
         hx, hy, hz = strip[3:6]
         y_hx, y_hz = turn(hx, 1, 1), turn(hz, 1, 1)
         z_hx, z_hy = strip_neighbours(False, 2 * instant, hx, hy)
@@ -650,9 +695,14 @@
     total = [None] * depth
     merge(True, 0)
     merge(True, 1)
-    strip_shifts, mixed = strip_shifted_electric(0)
-    moved = rolled_after(mixed, list(own))
-    strip_shifts, mixed = strip_magnetic(0)
+    at_last = group == last
+    strip[3] = jnp.where(at_last, strip[3] + turn(late_strips[True], GROUP * (last - 1), 1), strip[3])
+    strip[4] = jnp.where(at_last, strip[4] - turn(late_strips[True], GROUP * last, 1), strip[4])
+    main[3, last] = main[3, last] + trace(True, 1)
+    main[4, last] = main[4, last] - trace(True, 0)
+    strip_shifts, mixed = strip_shifted_magnetic(0)
+    moved = {p: (shifted[0, p - first + 1], shifted[1, p - first + 1]) for p in range(first - 1, last)}
+    moved[last + 1] = (zero, zero)
     for instant in range(HALO):
         item = 2 * instant
         final = instant == HALO - 1
@@ -662,25 +712,28 @@
             strip_shifts, mixed = strip_electric(instant)
         merge(False, item)
         merge(False, item + 1)
-        following = electric_planes(instant)
-        later = {p: (zero, zero) for p in following}
-        for planes in in_groups(magnetic_planes(instant)):
-            for p in planes:
-                z_ex, z_ey = main[0, p + 1], main[1, p + 1]
-                if p == last:
-                    z_ex, z_ey = z_ex + trace(True, item), z_ey + trace(True, item + 1)
-                curl = curl_of_electric(
-                    main[0, p], main[1, p], main[2, p], *moved.get(p, (zero, zero)), z_ex, z_ey
-                )
-                for c in range(3):
-                    main[3 + c, p] = main[3 + c, p] - (curl[c] if p >= first else below_factor * curl[c])
+        if instant == 0:
+            moved.update(rolled_before(main, mixed_now, [last], lane))
+        else:
+            following = electric_planes(instant)
+            later = {p: (zero, zero) for p in following}
+            for planes in in_groups(magnetic_planes(instant)):
+                for p in planes:
+                    z_ex, z_ey = main[0, p + 1], main[1, p + 1]
+                    if p == last:
+                        z_ex, z_ey = z_ex + trace(True, item), z_ey + trace(True, item + 1)
+                    curl = curl_of_electric(
+                        main[0, p], main[1, p], main[2, p], *moved.get(p, (zero, zero)), z_ex, z_ey
+                    )
+                    for c in range(3):
+                        main[3 + c, p] = main[3 + c, p] - (curl[c] if p >= first else below_factor * curl[c])
+                        if final and first <= p <= last:
+                            results[3 + c, p - first] = main[3 + c, p][0:rows] * COURANT
                     if final and first <= p <= last:
-                        results[3 + c, p - first] = main[3 + c, p][0:rows] * COURANT
-                if final and first <= p <= last:
-                    z = p - first
-                    hand_out(results.at[pl.ds(3, 3), z], fields_out.at[pl.ds(3, 3), z])
-            later.update(rolled_before(mixed_now, [p for p in planes if p in following]))
-        moved = later
+                        z = p - first
+                        hand_out(results.at[pl.ds(3, 3), z], fields_out.at[pl.ds(3, 3), z])
+                later.update(rolled_before(main, mixed_now, [p for p in planes if p in following], lane))
+            moved = later
 
         mixed_now = mixed
         if not final:
@@ -712,7 +765,7 @@
                     grad[z] = jnp.where(material[z] >= 2, -total[z], 0.0)
                     hand_out(results.at[pl.ds(0, 3), z], fields_out.at[pl.ds(0, 3), z])
                     hand_out(grad.at[z], eps_grad.at[z])
-            later.update(rolled_after(mixed_now, [p for p in planes if p in following]))
+            later.update(rolled_after(main, mixed_now, [p for p in planes if p in following], lane))
         moved = later
     for copy in copies:
         copy.wait()
@@ -765,15 +818,16 @@
     tiles = (slabs + 1) // 2
 
     inputs = (fields_in, material, source_profile, material_eps, source_wave)
-    to_a, to_b, scalars, fields_in, material, source_profile = call(
+    to_a, to_b, scalars, material, source_profile = call(
         x_pack_kernel,
         [far_off(array) for array in inputs],
         [(tiles, TILE, lanes)] * 2
-        + [(HALO + material_eps.shape[0], lanes), fields_in.shape, material, source_profile.shape],
+        + [(HALO + material_eps.shape[0], lanes), material, source_profile.shape],
         [
+            (2, 6, depth, TILE, lanes),
             pltpu.SMEM(material_eps.shape, F32),
             pltpu.SMEM(source_wave.shape, F32),
-            pltpu.SemaphoreType.DMA((5,)),
+            pltpu.SemaphoreType.DMA((6,)),
         ],
         name="x_pack",
     )
@@ -836,16 +890,17 @@
         name="arrived",
         cost=pl.CostEstimate(flops=10**9, bytes_accessed=0, transcendentals=0),
     )
-    strips, early_b = call(
+    strips, magnetic, shifted, early_b = call(
         prepare_kernel,
-        [strips, early_b],
-        [(8, wide, lanes), early_b.shape],
-        aliases={1: 1},
+        [fields_in, halo, strips, early_b],
+        [(8, wide, lanes), (3, depth + 2, wide, lanes), (2, depth, wide, lanes), early_b.shape],
+        aliases={3: 3},
         name="prepare",
     )
     fields_out, eps_grad = call(
         window_kernel,
-        [fields_in, coef, source_profile, halo, table, strips, early_a, early_b, late_a, late_b]
+        [fields_in, coef, source_profile, halo, table, strips, magnetic, shifted]
+        + [early_a, early_b, late_a, late_b]
         + [forward_fields, material],
         [(6, depth, rows, lanes), (depth, rows, lanes)],
         [

time: 22.6 us -> 21.9 us (0.969)
  waiting for transfers between devices: 3.51 us -> 3.14 us
  Pallas kernels: 7.95 us -> 7.61 us
    ppermute x1, waiting for transfers between devices: 2.89 us -> 2.52 us  [on_device(): late_a = lax.ppermute(late_a, ('gz', 'gx'), z_a)]
    pallas_call x8, Pallas kernels: 7.95 us -> 7.61 us  [call(): pl.pallas_call(kernel, out_shape=[jax.ShapeDtypeStruct(s, F32) for s in o...]
  transfers between devices with their start and end apart: 7 -> 7, of which waited for: 2 -> 2; matrix products, arithmetic and copies ran while one was open for 0% -> 0% of each run, Pallas kernels for 13% -> 16%
where the time goes in v3:
time: 21.9 us; the launch traced here: 21.7 us
  starting transfers between devices  9.56 us (44%)
  Pallas kernels  7.61 us (35%)
  waiting for transfers between devices  3.14 us (14%)
  between operations  1.38 us (6%)
    pallas_call x8, Pallas kernels, call(): pl.pallas_call(kernel, out_shape=[jax.ShapeDtypeStruct(s, F32) for s in o...  7.61 us
    ppermute x1, starting transfers between devices, on_device(): from_b = lax.ppermute(to_b, 'gx', swap_b)  2.64 us
    ppermute x1, starting transfers between devices, on_device(): early_a = lax.ppermute(early_a, ('gz', 'gx'), z_a)  2.58 us
    ppermute x1, waiting for transfers between devices, on_device(): late_a = lax.ppermute(late_a, ('gz', 'gx'), z_a)  2.52 us
    ppermute x1, starting transfers between devices, on_device(): late_a = lax.ppermute(late_a, ('gz', 'gx'), z_a)  2.23 us
    ppermute x1, starting transfers between devices, on_device(): both = lax.ppermute(y_out, 'gy', swap_a)  1.47 us
    ppermute x1, waiting for transfers between devices, on_device(): from_b = lax.ppermute(to_b, 'gx', swap_b)  0.61 us
    ppermute x1, starting transfers between devices, on_device(): from_a = lax.ppermute(to_a, 'gx', swap_a)  0.52 us
  transfers between devices with their start and end apart: 7, of which 2 were waited for; matrix products, arithmetic and copies ran while one was open for 0% of the time, Pallas kernels for 16%

profile of v3, /device:TPU:0, one launch (start us, length us, event | category | flops | bytes accessed | tf_op | source)
XLA Modules:
  0.0 21.7 jit_solution(5690396305862088252)
XLA Ops:
  0.6 0.0 copy-start
  0.6 1.2 %x_pack.1 = (f32[15,8,128]{2,1,0:T(8,128)S(1)}, f32[15,8,128]{2,1,0:T(8,128)S(1)}, f32[8,128]{1,0:T(8,128)S(1)}, s32[4,64,128]{2,1,0:T(8,128)S(1)}, f32[64,128]{1,0:T(8,128)S(1)}) custom-call(f32[6,4,64,128]{3,2,1,0:T(8,128)} %fields.11, s32[4,64,128]{2,1,0:T(8,128)} %material.1, f32[64,128]{1,0:T(8,128)} %profile.1, f32[4]{0:T(128)} %eps.1, f32[4]{0:T(128)} %wave.1), custom_call_target="tpu_custom_call" | custom-call | tf_op jit(solution)/shard_map/x_pack/pallas_call | solution.py:795
  1.8 0.5 %collective-permute-start = (f32[15,8,128]{2,1,0:T(8,128)S(1)}, f32[15,8,128]{2,1,0:T(8,128)S(1)}, u32[]{:S(2)}, u32[]{:S(2)}) collective-permute-start(f32[15,8,128]{2,1,0:T(8,128)S(1)} %get-tuple-element.25), channel_id=1, source_target_pairs={{0,2},{4,6},{2,0},{6,4},{1,3},{5,7},{3,1},{7,5},{8,10},{12,14},{10... | collective-permute-start | bytes 184328 | tf_op jit(solution)/shard_map/ppermute | solution.py:835
  2.3 2.6 %collective-permute-start.1 = (f32[15,8,128]{2,1,0:T(8,128)S(1)}, f32[15,8,128]{2,1,0:T(8,128)S(1)}, u32[]{:S(2)}, u32[]{:S(2)}) collective-permute-start(f32[15,8,128]{2,1,0:T(8,128)S(1)} %get-tuple-element.26), channel_id=1, source_target_pairs={{2,4},{6,0},{4,2},{0,6},{3,5},{7,1},{5,3},{1,7},{10,12},{14,8},{12... | collective-permute-start | bytes 184328 | tf_op jit(solution)/shard_map/ppermute | solution.py:836
  5.7 0.0 copy-done
  5.7 0.9 %interior.1 = (f32[4,64,128]{2,1,0:T(8,128)S(1)}, f32[488,128]{1,0:T(8,128)S(1)}, f32[616,128]{1,0:T(8,128)S(1)}, f32[2,72,128]{2,1,0:T(8,128)S(1)}, f32[28,128]{1,0:T(8,128)S(1)}) custom-call(f32[6,4,64,128]{3,2,1,0:T(8,128)S(1)} %copy-done, s32[4,64,128]{2,1,0:T(8,128)S(1)} %get-tuple-element.21.material, f32[64,128]{1,0:T(8,128)S(1)} %get-tuple-element.22.profile, ...), custom_call_target="tpu_custom_call" | custom-call | tf_op jit(solution)/shard_map/interior/pallas_call | solution.py:795
  6.5 0.1 collective-permute-start.3
  6.7 0.0 collective-permute-done.from_a
  6.7 0.6 %collective-permute-done.1.from_b = f32[15,8,128]{2,1,0:T(8,128)S(1)} collective-permute-done((f32[15,8,128]{2,1,0:T(8,128)S(1)}, f32[15,8,128]{2,1,0:T(8,128)S(1)}, u32[]{:S(2)}, u32[]{:S(2)}) %collective-permute-start.1) | collective-permute-done | bytes 61472 | tf_op jit(solution)/shard_map/ppermute | solution.py:836
  7.3 0.1 x_unpack.1
  7.4 1.5 %collective-permute-start.2 = (f32[2,72,128]{2,1,0:T(8,128)S(1)}, f32[2,72,128]{2,1,0:T(8,128)S(1)}, u32[]{:S(2)}, u32[]{:S(2)}) collective-permute-start(f32[2,72,128]{2,1,0:T(8,128)S(1)} %get-tuple-element.30), channel_id=1, source_target_pairs={{0,1},{1,0},{2,3},{3,2},{4,5},{5,4},{6,7},{7,6},{8,9},{9,8},{10,11... | collective-permute-start | bytes 221192 | tf_op jit(solution)/shard_map/ppermute | solution.py:859
  8.9 2.6 %collective-permute-start.4 = (f32[488,128]{1,0:T(8,128)S(1)}, f32[488,128]{1,0:T(8,128)S(1)}, u32[]{:S(2)}, u32[]{:S(2)}) collective-permute-start(f32[488,128]{1,0:T(8,128)S(1)} %get-tuple-element.36), channel_id=1, source_target_pairs={{0,8},{2,10},{4,12},{6,14},{16,24},{18,26},{20,28},{22,30},{8,0},{... | collective-permute-start | bytes 749576 | tf_op jit(solution)/shard_map/ppermute | solution.py:865
  11.4 0.7 %own_strips.1.own = f32[8,72,128]{2,1,0:T(8,128)S(1)} custom-call(f32[6,4,64,128]{3,2,1,0:T(8,128)S(1)} %copy-done, f32[4,64,128]{2,1,0:T(8,128)S(1)} %get-tuple-element.24.coef, f32[64,128]{1,0:T(8,128)S(1)} %get-tuple-element.22.profile, f32[29,8,128]{2,1,0:T(8,128)S(1)} %get-tuple-element.28.halo), custom_call_target="tpu_custom_call" | custom-call | tf_op jit(solution)/shard_map/own_strips/pallas_call | solution.py:795
  12.1 0.0 collective-permute-done.2
  12.1 1.0 %frame.1 = (f32[8,72,128]{2,1,0:T(8,128)S(1)}, f32[136,128]{1,0:T(8,128)S(1)}, f32[176,128]{1,0:T(8,128)S(1)}) custom-call(f32[6,4,64,128]{3,2,1,0:T(8,128)S(1)} %copy-done, f32[4,64,128]{2,1,0:T(8,128)S(1)} %get-tuple-element.24.coef, f32[64,128]{1,0:T(8,128)S(1)} %get-tuple-element.22.profile, f32[28,128]{1,0:T(8,128)S(1)} %get-tuple-element.29.table, ...), custom_call_target="tpu_custom_call" | custom-call | tf_op jit(solution)/shard_map/frame/pallas_call | solution.py:795
  13.1 2.2 %collective-permute-start.5 = (f32[136,128]{1,0:T(8,128)S(1)}, f32[136,128]{1,0:T(8,128)S(1)}, u32[]{:S(2)}, u32[]{:S(2)}) collective-permute-start(f32[136,128]{1,0:T(8,128)S(1)} %get-tuple-element.38), channel_id=1, source_target_pairs={{0,8},{2,10},{4,12},{6,14},{16,24},{18,26},{20,28},{22,30},{8,0},{... | collective-permute-start | bytes 208904 | tf_op jit(solution)/shard_map/ppermute | solution.py:882
  15.3 0.0 collective-permute-start.6
  15.3 0.0 collective-permute-done.3.refs_0_
  15.3 0.8 %prepare.1 = (f32[8,72,128]{2,1,0:T(8,128)S(1)}, f32[3,6,72,128]{3,2,1,0:T(8,128)S(1)}, f32[2,4,72,128]{3,2,1,0:T(8,128)S(1)}, f32[616,128]{1,0:T(8,128)S(1)}) custom-call(f32[6,4,64,128]{3,2,1,0:T(8,128)S(1)} %copy-done, f32[29,8,128]{2,1,0:T(8,128)S(1)} %get-tuple-element.28.halo, ...), custom_call_target="tpu_custom_call", output_to_operand_aliasing={{3}: (3, {})} | custom-call | tf_op jit(solution)/shard_map/prepare/pallas_call | solution.py:795
  16.1 2.5 %collective-permute-done.5.late_a = f32[136,128]{1,0:T(8,128)S(1)} collective-permute-done((f32[136,128]{1,0:T(8,128)S(1)}, f32[136,128]{1,0:T(8,128)S(1)}, u32[]{:S(2)}, u32[]{:S(2)}) %collective-permute-start.5) | collective-permute-done | bytes 69664 | tf_op jit(solution)/shard_map/ppermute | solution.py:882
  18.6 0.0 collective-permute-done.6.late_b
  18.6 0.0 collective-permute-done.4.early_a
  18.6 0.0 copy-done.1
  18.6 3.1 %window.1 = (f32[6,4,64,128]{3,2,1,0:T(8,128)}, f32[4,64,128]{2,1,0:T(8,128)}) custom-call(f32[6,4,64,128]{3,2,1,0:T(8,128)S(1)} %copy-done, f32[4,64,128]{2,1,0:T(8,128)S(1)} %get-tuple-element.24.coef, f32[64,128]{1,0:T(8,128)S(1)} %get-tuple-element.22.profile, f32[29,8,128]{2,1,0:T(8,128)S(1)} %get-tuple-element.28.halo, ...), custom_call_target="tpu_custom_call" | custom-call | tf_op jit(solution)/shard_map/window/pallas_call | solution.py:795
  (4 shorter events, 0.0 us)
Async XLA Ops:
  0.6 5.0 %copy-start = (f32[6,4,64,128]{3,2,1,0:T(8,128)S(1)}, f32[6,4,64,128]{3,2,1,0:T(8,128)}, u32[]{:S(2)}) copy-start(f32[6,4,64,128]{3,2,1,0:T(8,128)} %fields.11) | copy-start | bytes 2359300
  1.8 4.8 %collective-permute-start = (f32[15,8,128]{2,1,0:T(8,128)S(1)}, f32[15,8,128]{2,1,0:T(8,128)S(1)}, u32[]{:S(2)}, u32[]{:S(2)}) collective-permute-start(f32[15,8,128]{2,1,0:T(8,128)S(1)} %get-tuple-element.25), channel_id=1, source_target_pairs={{0,2},{4,6},{2,0},{6,4},{1,3},{5,7},{3,1},{7,5},{8,10},{12,14},{10... | collective-permute-start | bytes 184328 | tf_op jit(solution)/shard_map/ppermute | solution.py:835
  2.3 4.9 %collective-permute-start.1 = (f32[15,8,128]{2,1,0:T(8,128)S(1)}, f32[15,8,128]{2,1,0:T(8,128)S(1)}, u32[]{:S(2)}, u32[]{:S(2)}) collective-permute-start(f32[15,8,128]{2,1,0:T(8,128)S(1)} %get-tuple-element.26), channel_id=1, source_target_pairs={{2,4},{6,0},{4,2},{0,6},{3,5},{7,1},{5,3},{1,7},{10,12},{14,8},{12... | collective-permute-start | bytes 184328 | tf_op jit(solution)/shard_map/ppermute | solution.py:836
  6.5 8.8 %collective-permute-start.3 = (f32[616,128]{1,0:T(8,128)S(1)}, f32[616,128]{1,0:T(8,128)S(1)}, u32[]{:S(2)}, u32[]{:S(2)}) collective-permute-start(f32[616,128]{1,0:T(8,128)S(1)} %get-tuple-element.32), channel_id=1, source_target_pairs={{8,16},{10,18},{12,20},{14,22},{16,8},{18,10},{20,12},{22,14},{0,2... | collective-permute-start | bytes 946184 | tf_op jit(solution)/shard_map/ppermute | solution.py:866
  7.4 4.7 %collective-permute-start.2 = (f32[2,72,128]{2,1,0:T(8,128)S(1)}, f32[2,72,128]{2,1,0:T(8,128)S(1)}, u32[]{:S(2)}, u32[]{:S(2)}) collective-permute-start(f32[2,72,128]{2,1,0:T(8,128)S(1)} %get-tuple-element.30), channel_id=1, source_target_pairs={{0,1},{1,0},{2,3},{3,2},{4,5},{5,4},{6,7},{7,6},{8,9},{9,8},{10,11... | collective-permute-start | bytes 221192 | tf_op jit(solution)/shard_map/ppermute | solution.py:859
  8.9 9.8 %collective-permute-start.4 = (f32[488,128]{1,0:T(8,128)S(1)}, f32[488,128]{1,0:T(8,128)S(1)}, u32[]{:S(2)}, u32[]{:S(2)}) collective-permute-start(f32[488,128]{1,0:T(8,128)S(1)} %get-tuple-element.36), channel_id=1, source_target_pairs={{0,8},{2,10},{4,12},{6,14},{16,24},{18,26},{20,28},{22,30},{8,0},{... | collective-permute-start | bytes 749576 | tf_op jit(solution)/shard_map/ppermute | solution.py:865
  13.1 5.5 %collective-permute-start.5 = (f32[136,128]{1,0:T(8,128)S(1)}, f32[136,128]{1,0:T(8,128)S(1)}, u32[]{:S(2)}, u32[]{:S(2)}) collective-permute-start(f32[136,128]{1,0:T(8,128)S(1)} %get-tuple-element.38), channel_id=1, source_target_pairs={{0,8},{2,10},{4,12},{6,14},{16,24},{18,26},{20,28},{22,30},{8,0},{... | collective-permute-start | bytes 208904 | tf_op jit(solution)/shard_map/ppermute | solution.py:882
  15.3 3.3 %collective-permute-start.6 = (f32[176,128]{1,0:T(8,128)S(1)}, f32[176,128]{1,0:T(8,128)S(1)}, u32[]{:S(2)}, u32[]{:S(2)}) collective-permute-start(f32[176,128]{1,0:T(8,128)S(1)} %get-tuple-element.39), channel_id=1, source_target_pairs={{8,16},{10,18},{12,20},{14,22},{16,8},{18,10},{20,12},{22,14},{0,2... | collective-permute-start | bytes 270344 | tf_op jit(solution)/shard_map/ppermute | solution.py:883
  15.3 3.3 %copy-start.1 = (bf16[4,3,4,64,128]{4,3,2,1,0:T(8,128)(2,1)S(1)}, bf16[4,3,4,64,128]{4,3,2,1,0:T(8,128)(2,1)}, u32[]{:S(2)}) copy-start(bf16[4,3,4,64,128]{4,3,2,1,0:T(8,128)(2,1)} %forward.1) | copy-start | bytes 2359300

commit v4 on v3

--- a/solution.py
+++ b/solution.py
@@ -395,8 +395,11 @@
         for c in range(2):
             item = 2 * instant + c
             here = lane // GROUP == item
-            upward = jnp.where(here, turn(strip[3 + c], GROUP * item - WIDE * (depth - 1) - TILE, 1), upward)
-            downward = jnp.where(here, turn(electric[c], GROUP * item - TILE, 1), downward)
+            both = jnp.where(lane < lanes // 2, electric[c], strip[3 + c])
+            both = turn(both, GROUP * item - WIDE * (depth - 1) - TILE, 1)
+            upward = jnp.where(here, both, upward)
+            there = lane // GROUP == (item - WIDE * (depth - 1) // GROUP) % TRACES
+            downward = jnp.where(there, both, downward)
     to_a[0:wide, :] = jnp.where(even, upward, downward)
     to_b[0:wide, :] = jnp.where(even, downward, upward)
     def send(at, up, down):
@@ -488,7 +491,9 @@
     return jnp.concatenate([own, halo[depth * c + z]], axis=0)
 
 
-def prepare_kernel(fields, halo, wide_strips, early, strips, magnetic, shifted, out):
+def prepare_kernel(
+    fields, halo, coef, profile, table, wide_strips, early, strips, magnetic, shifted, electric, shifted_on, inner, shifted_inner, out
+):
     _, wide, lanes = wide_strips.shape
     depth = lanes // WIDE
     first, last = BEYOND, BEYOND + depth - 1
@@ -526,6 +531,37 @@
     moved = rolled_before(main, mixed, range(first - 1, last), lane)
     for p in range(first - 1, last):
         shifted[0, p - first + 1], shifted[1, p - first + 1] = moved[p]
+    back = curl_of_magnetic(hx, hy, hz, turn(hx, 1, 1), turn(hz, 1, 1), turn(hx, GROUP, 1), turn(hy, GROUP, 1))
+    ex = ex + strips[6] * (back[0] + plane_amount(table, 0, depth + 1, depth) * strips[7])
+    ey = ey + strips[6] * back[1]
+    ez = ez + strips[6] * back[2]
+    y_ex, y_ez = turn(ex, -1, 1), turn(ez, -1, 1)
+    wide_profile = jnp.concatenate([profile[...], halo[7 * depth]], axis=0)
+    for p in range(first, last):
+        z = p - first
+        back = curl_of_magnetic(main[3, p], main[4, p], main[5, p], *moved[p], main[3, p - 1], main[4, p - 1])
+        back = (back[0] + plane_amount(table, 0, z, depth) * wide_profile, back[1], back[2])
+        here = jnp.concatenate([coef[z], halo[6 * depth + z]], axis=0)
+        for c in range(3):
+            main[c, p] = main[c, p] + here * back[c]
+            electric[c, z] = main[c, p]
+    between = range(first + 1, last)
+    moved = rolled_after(main, edges_after(y_ex, ez, lane), between, lane)
+    for p in between:
+        shifted_on[0, p - first - 1], shifted_on[1, p - first - 1] = moved[p]
+    curl = curl_of_electric(ex, ey, ez, y_ex, y_ez, turn(ex, -GROUP, 1), turn(ey, -GROUP, 1))
+    hx, hz = hx - strip_factor * curl[0], hz - strip_factor * curl[2]
+    for p in range(first + 1, last - 1):
+        curl = curl_of_electric(
+            main[0, p], main[1, p], main[2, p], *moved[p], main[0, p + 1], main[1, p + 1]
+        )
+        for c in range(3):
+            main[3 + c, p] = main[3 + c, p] - curl[c]
+            inner[c, p - first - 1] = main[3 + c, p]
+    mixed = edges_before(turn(hx, 1, 1), hz, lane)
+    moved = rolled_before(main, mixed, range(first + 1, last - 1), lane)
+    for p in range(first + 1, last - 1):
+        shifted_inner[0, p - first - 1], shifted_inner[1, p - first - 1] = moved[p]
 
 
 def window_kernel(
@@ -537,6 +573,10 @@
     strips,
     magnetic,
     shifted,
+    electric,
+    shifted_on,
+    inner,
+    shifted_inner,
     early_a,
     early_b,
     late_a,
@@ -559,6 +599,7 @@
     group = lane // GROUP
 
     late_strips = [received(late_a, late_b, above, slice(0, wide)) for above in (False, True)]
+    late_strips[True] = turn(late_strips[True], WIDE * (depth - 1), 1)
     places, early_end = early_rows(rows)
     traces = {}
 
@@ -712,6 +753,7 @@
             strip_shifts, mixed = strip_electric(instant)
         merge(False, item)
         merge(False, item + 1)
+        ready = range(first + 1, last - 1) if instant == 1 else ()
         if instant == 0:
             moved.update(rolled_before(main, mixed_now, [last], lane))
         else:
@@ -719,6 +761,11 @@
             later = {p: (zero, zero) for p in following}
             for planes in in_groups(magnetic_planes(instant)):
                 for p in planes:
+                    if p in ready:
+                        for c in range(3):
+                            main[3 + c, p] = inner[c, p - first - 1]
+                        later[p] = (shifted_inner[0, p - first - 1], shifted_inner[1, p - first - 1])
+                        continue
                     z_ex, z_ey = main[0, p + 1], main[1, p + 1]
                     if p == last:
                         z_ex, z_ey = z_ex + trace(True, item), z_ey + trace(True, item + 1)
@@ -732,7 +779,7 @@
                     if final and first <= p <= last:
                         z = p - first
                         hand_out(results.at[pl.ds(3, 3), z], fields_out.at[pl.ds(3, 3), z])
-                later.update(rolled_before(main, mixed_now, [p for p in planes if p in following], lane))
+                later.update(rolled_before(main, mixed_now, [p for p in planes if p in following and p not in ready], lane))
             moved = later
 
         mixed_now = mixed
@@ -747,15 +794,21 @@
                 z_hx, z_hy = main.get((3, p - 1), zero), main.get((4, p - 1), zero)
                 if p == first:
                     z_hx, z_hy = z_hx + trace(False, item), z_hy + trace(False, item + 1)
-                back = curl_of_magnetic(main[3, p], main[4, p], main[5, p], *moved[p], z_hx, z_hy)
                 here = wide_coef[p]
                 inside = first <= p <= last
                 z = p - first
-                if inside:
+                there = instant == 0 and first <= p < last
+                back = None
+                if not there:
+                    back = curl_of_magnetic(main[3, p], main[4, p], main[5, p], *moved[p], z_hx, z_hy)
+                if inside and not there:
                     push = plane_amount(table, instant, z, depth) * wide_profile
                     back = (back[0] + push, back[1], back[2])
                 for c in range(3):
-                    main[c, p] = main[c, p] + here * back[c]
+                    main[c, p] = electric[c, z] if there else main[c, p] + here * back[c]
+                    if there and p == first and c < 2:
+                        enters = here * trace(False, item + 1 - c)
+                        main[c, p] = main[c, p] + enters if c == 0 else main[c, p] - enters
                     if inside:
                         term = forward[instant, c, z].astype(F32) * main[c, p][0:rows]
                         total[z] = term if total[z] is None else total[z] + term
@@ -765,7 +818,11 @@
                     grad[z] = jnp.where(material[z] >= 2, -total[z], 0.0)
                     hand_out(results.at[pl.ds(0, 3), z], fields_out.at[pl.ds(0, 3), z])
                     hand_out(grad.at[z], eps_grad.at[z])
-            later.update(rolled_after(main, mixed_now, [p for p in planes if p in following], lane))
+            given = [p for p in planes if instant == 0 and first < p < last]
+            later.update(
+                rolled_after(main, mixed_now, [p for p in planes if p in following and p not in given], lane)
+            )
+            later.update({p: (shifted_on[0, p - first - 1], shifted_on[1, p - first - 1]) for p in given})
         moved = later
     for copy in copies:
         copy.wait()
@@ -890,16 +947,17 @@
         name="arrived",
         cost=pl.CostEstimate(flops=10**9, bytes_accessed=0, transcendentals=0),
     )
-    strips, magnetic, shifted, early_b = call(
+    strips, *prepared, early_b = call(
         prepare_kernel,
-        [fields_in, halo, strips, early_b],
-        [(8, wide, lanes), (3, depth + 2, wide, lanes), (2, depth, wide, lanes), early_b.shape],
-        aliases={3: 3},
+        [fields_in, halo, coef, source_profile, table, strips, early_b],
+        [(8, wide, lanes), (3, depth + 2, wide, lanes), (2, depth, wide, lanes), (3, depth - 1, wide, lanes)]
+        + [(2, depth - 2, wide, lanes), (3, depth - 3, wide, lanes), (2, depth - 3, wide, lanes), early_b.shape],
+        aliases={6: 7},
         name="prepare",
     )
     fields_out, eps_grad = call(
         window_kernel,
-        [fields_in, coef, source_profile, halo, table, strips, magnetic, shifted]
+        [fields_in, coef, source_profile, halo, table, strips, *prepared]
         + [early_a, early_b, late_a, late_b]
         + [forward_fields, material],
         [(6, depth, rows, lanes), (depth, rows, lanes)],

time: 21.9 us -> 22 us (level)
  Pallas kernels: 7.61 us -> 8.12 us
  waiting for transfers between devices: 3.14 us -> 2.72 us
    pallas_call x8, Pallas kernels: 7.61 us -> 8.12 us  [call(): pl.pallas_call(kernel, out_shape=[jax.ShapeDtypeStruct(s, F32) for s in o...]
    ppermute x1, waiting for transfers between devices: 2.52 us -> 2.11 us  [on_device(): late_a = lax.ppermute(late_a, ('gz', 'gx'), z_a)]
  transfers between devices with their start and end apart: 7 -> 7, of which waited for: 2 -> 2; matrix products, arithmetic and copies ran while one was open for 0% -> 0% of each run, Pallas kernels for 16% -> 17%
where the time goes in v4:
time: 22 us; the launch traced here: 21.8 us
  starting transfers between devices  9.57 us (44%)
  Pallas kernels  8.12 us (37%)
  waiting for transfers between devices  2.72 us (12%)
  between operations  1.38 us (6%)
    pallas_call x8, Pallas kernels, call(): pl.pallas_call(kernel, out_shape=[jax.ShapeDtypeStruct(s, F32) for s in o...  8.12 us
    ppermute x1, starting transfers between devices, on_device(): from_b = lax.ppermute(to_b, 'gx', swap_b)  2.64 us
    ppermute x1, starting transfers between devices, on_device(): early_a = lax.ppermute(early_a, ('gz', 'gx'), z_a)  2.59 us
    ppermute x1, starting transfers between devices, on_device(): late_a = lax.ppermute(late_a, ('gz', 'gx'), z_a)  2.23 us
    ppermute x1, waiting for transfers between devices, on_device(): late_a = lax.ppermute(late_a, ('gz', 'gx'), z_a)  2.11 us
    ppermute x1, starting transfers between devices, on_device(): both = lax.ppermute(y_out, 'gy', swap_a)  1.47 us
    ppermute x1, waiting for transfers between devices, on_device(): from_b = lax.ppermute(to_b, 'gx', swap_b)  0.6 us
    ppermute x1, starting transfers between devices, on_device(): from_a = lax.ppermute(to_a, 'gx', swap_a)  0.52 us
  transfers between devices with their start and end apart: 7, of which 2 were waited for; matrix products, arithmetic and copies ran while one was open for 0% of the time, Pallas kernels for 17%

profile of v4, /device:TPU:0, one launch (start us, length us, event | category | flops | bytes accessed | tf_op | source)
XLA Modules:
  0.0 21.8 jit_solution(2125248006260842162)
XLA Ops:
  0.6 0.0 copy-start
  0.6 1.2 %x_pack.1 = (f32[15,8,128]{2,1,0:T(8,128)S(1)}, f32[15,8,128]{2,1,0:T(8,128)S(1)}, f32[8,128]{1,0:T(8,128)S(1)}, s32[4,64,128]{2,1,0:T(8,128)S(1)}, f32[64,128]{1,0:T(8,128)S(1)}) custom-call(f32[6,4,64,128]{3,2,1,0:T(8,128)} %fields.11, s32[4,64,128]{2,1,0:T(8,128)} %material.1, f32[64,128]{1,0:T(8,128)} %profile.1, f32[4]{0:T(128)} %eps.1, f32[4]{0:T(128)} %wave.1), custom_call_target="tpu_custom_call" | custom-call | tf_op jit(solution)/shard_map/x_pack/pallas_call | solution.py:852
  1.8 0.5 %collective-permute-start = (f32[15,8,128]{2,1,0:T(8,128)S(1)}, f32[15,8,128]{2,1,0:T(8,128)S(1)}, u32[]{:S(2)}, u32[]{:S(2)}) collective-permute-start(f32[15,8,128]{2,1,0:T(8,128)S(1)} %get-tuple-element.29), channel_id=1, source_target_pairs={{0,2},{4,6},{2,0},{6,4},{1,3},{5,7},{3,1},{7,5},{8,10},{12,14},{10... | collective-permute-start | bytes 184328 | tf_op jit(solution)/shard_map/ppermute | solution.py:892
  2.3 2.6 %collective-permute-start.1 = (f32[15,8,128]{2,1,0:T(8,128)S(1)}, f32[15,8,128]{2,1,0:T(8,128)S(1)}, u32[]{:S(2)}, u32[]{:S(2)}) collective-permute-start(f32[15,8,128]{2,1,0:T(8,128)S(1)} %get-tuple-element.30), channel_id=1, source_target_pairs={{2,4},{6,0},{4,2},{0,6},{3,5},{7,1},{5,3},{1,7},{10,12},{14,8},{12... | collective-permute-start | bytes 184328 | tf_op jit(solution)/shard_map/ppermute | solution.py:893
  5.7 0.0 copy-done
  5.7 0.9 %interior.1 = (f32[4,64,128]{2,1,0:T(8,128)S(1)}, f32[488,128]{1,0:T(8,128)S(1)}, f32[616,128]{1,0:T(8,128)S(1)}, f32[2,72,128]{2,1,0:T(8,128)S(1)}, f32[28,128]{1,0:T(8,128)S(1)}) custom-call(f32[6,4,64,128]{3,2,1,0:T(8,128)S(1)} %copy-done, s32[4,64,128]{2,1,0:T(8,128)S(1)} %get-tuple-element.25.material, f32[64,128]{1,0:T(8,128)S(1)} %get-tuple-element.26.profile, ...), custom_call_target="tpu_custom_call" | custom-call | tf_op jit(solution)/shard_map/interior/pallas_call | solution.py:852
  6.5 0.1 collective-permute-start.3
  6.7 0.0 collective-permute-done.from_a
  6.7 0.6 %collective-permute-done.1.from_b = f32[15,8,128]{2,1,0:T(8,128)S(1)} collective-permute-done((f32[15,8,128]{2,1,0:T(8,128)S(1)}, f32[15,8,128]{2,1,0:T(8,128)S(1)}, u32[]{:S(2)}, u32[]{:S(2)}) %collective-permute-start.1) | collective-permute-done | bytes 61472 | tf_op jit(solution)/shard_map/ppermute | solution.py:893
  7.3 0.1 x_unpack.1
  7.4 1.5 %collective-permute-start.2 = (f32[2,72,128]{2,1,0:T(8,128)S(1)}, f32[2,72,128]{2,1,0:T(8,128)S(1)}, u32[]{:S(2)}, u32[]{:S(2)}) collective-permute-start(f32[2,72,128]{2,1,0:T(8,128)S(1)} %get-tuple-element.34), channel_id=1, source_target_pairs={{0,1},{1,0},{2,3},{3,2},{4,5},{5,4},{6,7},{7,6},{8,9},{9,8},{10,11... | collective-permute-start | bytes 221192 | tf_op jit(solution)/shard_map/ppermute | solution.py:916
  8.9 2.6 %collective-permute-start.4 = (f32[488,128]{1,0:T(8,128)S(1)}, f32[488,128]{1,0:T(8,128)S(1)}, u32[]{:S(2)}, u32[]{:S(2)}) collective-permute-start(f32[488,128]{1,0:T(8,128)S(1)} %get-tuple-element.44), channel_id=1, source_target_pairs={{0,8},{2,10},{4,12},{6,14},{16,24},{18,26},{20,28},{22,30},{8,0},{... | collective-permute-start | bytes 749576 | tf_op jit(solution)/shard_map/ppermute | solution.py:922
  11.4 0.7 %own_strips.1.own = f32[8,72,128]{2,1,0:T(8,128)S(1)} custom-call(f32[6,4,64,128]{3,2,1,0:T(8,128)S(1)} %copy-done, f32[4,64,128]{2,1,0:T(8,128)S(1)} %get-tuple-element.28.coef, f32[64,128]{1,0:T(8,128)S(1)} %get-tuple-element.26.profile, f32[29,8,128]{2,1,0:T(8,128)S(1)} %get-tuple-element.32.halo), custom_call_target="tpu_custom_call" | custom-call | tf_op jit(solution)/shard_map/own_strips/pallas_call | solution.py:852
  12.1 0.0 collective-permute-done.2
  12.2 1.0 %frame.1 = (f32[8,72,128]{2,1,0:T(8,128)S(1)}, f32[136,128]{1,0:T(8,128)S(1)}, f32[176,128]{1,0:T(8,128)S(1)}) custom-call(f32[6,4,64,128]{3,2,1,0:T(8,128)S(1)} %copy-done, f32[4,64,128]{2,1,0:T(8,128)S(1)} %get-tuple-element.28.coef, f32[64,128]{1,0:T(8,128)S(1)} %get-tuple-element.26.profile, f32[28,128]{1,0:T(8,128)S(1)} %get-tuple-element.33.table, ...), custom_call_target="tpu_custom_call" | custom-call | tf_op jit(solution)/shard_map/frame/pallas_call | solution.py:852
  13.1 2.2 %collective-permute-start.5 = (f32[136,128]{1,0:T(8,128)S(1)}, f32[136,128]{1,0:T(8,128)S(1)}, u32[]{:S(2)}, u32[]{:S(2)}) collective-permute-start(f32[136,128]{1,0:T(8,128)S(1)} %get-tuple-element.46), channel_id=1, source_target_pairs={{0,8},{2,10},{4,12},{6,14},{16,24},{18,26},{20,28},{22,30},{8,0},{... | collective-permute-start | bytes 208904 | tf_op jit(solution)/shard_map/ppermute | solution.py:939
  15.4 0.0 collective-permute-start.6
  15.4 0.0 collective-permute-done.3.refs_0_
  15.4 1.2 %prepare.1 = (f32[8,72,128]{2,1,0:T(8,128)S(1)}, f32[3,6,72,128]{3,2,1,0:T(8,128)S(1)}, f32[2,4,72,128]{3,2,1,0:T(8,128)S(1)}, f32[3,3,72,128]{3,2,1,0:T(8,128)S...) custom-call(f32[6,4,64,128]{3,2,1,0:T(8,128)S(1)} %copy-done, ...), custom_call_target="tpu_custom_call", output_to_operand_aliasing={{7}: (6, {})} | custom-call | tf_op jit(solution)/shard_map/prepare/pallas_call | solution.py:852
  16.5 2.1 %collective-permute-done.5.late_a = f32[136,128]{1,0:T(8,128)S(1)} collective-permute-done((f32[136,128]{1,0:T(8,128)S(1)}, f32[136,128]{1,0:T(8,128)S(1)}, u32[]{:S(2)}, u32[]{:S(2)}) %collective-permute-start.5) | collective-permute-done | bytes 69664 | tf_op jit(solution)/shard_map/ppermute | solution.py:939
  18.6 0.0 collective-permute-done.6.late_b
  18.7 0.0 collective-permute-done.4.early_a
  18.7 0.0 copy-done.1
  18.7 3.1 %window.1 = (f32[6,4,64,128]{3,2,1,0:T(8,128)}, f32[4,64,128]{2,1,0:T(8,128)}) custom-call(f32[6,4,64,128]{3,2,1,0:T(8,128)S(1)} %copy-done, f32[4,64,128]{2,1,0:T(8,128)S(1)} %get-tuple-element.28.coef, f32[64,128]{1,0:T(8,128)S(1)} %get-tuple-element.26.profile, f32[29,8,128]{2,1,0:T(8,128)S(1)} %get-tuple-element.32.halo, ...), custom_call_target="tpu_custom_call" | custom-call | tf_op jit(solution)/shard_map/window/pallas_call | solution.py:852
  (4 shorter events, 0.0 us)
Async XLA Ops:
  0.6 5.0 %copy-start = (f32[6,4,64,128]{3,2,1,0:T(8,128)S(1)}, f32[6,4,64,128]{3,2,1,0:T(8,128)}, u32[]{:S(2)}) copy-start(f32[6,4,64,128]{3,2,1,0:T(8,128)} %fields.11) | copy-start | bytes 2359300
  1.8 4.9 %collective-permute-start = (f32[15,8,128]{2,1,0:T(8,128)S(1)}, f32[15,8,128]{2,1,0:T(8,128)S(1)}, u32[]{:S(2)}, u32[]{:S(2)}) collective-permute-start(f32[15,8,128]{2,1,0:T(8,128)S(1)} %get-tuple-element.29), channel_id=1, source_target_pairs={{0,2},{4,6},{2,0},{6,4},{1,3},{5,7},{3,1},{7,5},{8,10},{12,14},{10... | collective-permute-start | bytes 184328 | tf_op jit(solution)/shard_map/ppermute | solution.py:892
  2.3 4.9 %collective-permute-start.1 = (f32[15,8,128]{2,1,0:T(8,128)S(1)}, f32[15,8,128]{2,1,0:T(8,128)S(1)}, u32[]{:S(2)}, u32[]{:S(2)}) collective-permute-start(f32[15,8,128]{2,1,0:T(8,128)S(1)} %get-tuple-element.30), channel_id=1, source_target_pairs={{2,4},{6,0},{4,2},{0,6},{3,5},{7,1},{5,3},{1,7},{10,12},{14,8},{12... | collective-permute-start | bytes 184328 | tf_op jit(solution)/shard_map/ppermute | solution.py:893
  6.5 8.8 %collective-permute-start.3 = (f32[616,128]{1,0:T(8,128)S(1)}, f32[616,128]{1,0:T(8,128)S(1)}, u32[]{:S(2)}, u32[]{:S(2)}) collective-permute-start(f32[616,128]{1,0:T(8,128)S(1)} %get-tuple-element.36), channel_id=1, source_target_pairs={{8,16},{10,18},{12,20},{14,22},{16,8},{18,10},{20,12},{22,14},{0,2... | collective-permute-start | bytes 946184 | tf_op jit(solution)/shard_map/ppermute | solution.py:923
  7.4 4.7 %collective-permute-start.2 = (f32[2,72,128]{2,1,0:T(8,128)S(1)}, f32[2,72,128]{2,1,0:T(8,128)S(1)}, u32[]{:S(2)}, u32[]{:S(2)}) collective-permute-start(f32[2,72,128]{2,1,0:T(8,128)S(1)} %get-tuple-element.34), channel_id=1, source_target_pairs={{0,1},{1,0},{2,3},{3,2},{4,5},{5,4},{6,7},{7,6},{8,9},{9,8},{10,11... | collective-permute-start | bytes 221192 | tf_op jit(solution)/shard_map/ppermute | solution.py:916
  8.9 9.8 %collective-permute-start.4 = (f32[488,128]{1,0:T(8,128)S(1)}, f32[488,128]{1,0:T(8,128)S(1)}, u32[]{:S(2)}, u32[]{:S(2)}) collective-permute-start(f32[488,128]{1,0:T(8,128)S(1)} %get-tuple-element.44), channel_id=1, source_target_pairs={{0,8},{2,10},{4,12},{6,14},{16,24},{18,26},{20,28},{22,30},{8,0},{... | collective-permute-start | bytes 749576 | tf_op jit(solution)/shard_map/ppermute | solution.py:922
  13.1 5.5 %collective-permute-start.5 = (f32[136,128]{1,0:T(8,128)S(1)}, f32[136,128]{1,0:T(8,128)S(1)}, u32[]{:S(2)}, u32[]{:S(2)}) collective-permute-start(f32[136,128]{1,0:T(8,128)S(1)} %get-tuple-element.46), channel_id=1, source_target_pairs={{0,8},{2,10},{4,12},{6,14},{16,24},{18,26},{20,28},{22,30},{8,0},{... | collective-permute-start | bytes 208904 | tf_op jit(solution)/shard_map/ppermute | solution.py:939
  15.4 3.3 %collective-permute-start.6 = (f32[176,128]{1,0:T(8,128)S(1)}, f32[176,128]{1,0:T(8,128)S(1)}, u32[]{:S(2)}, u32[]{:S(2)}) collective-permute-start(f32[176,128]{1,0:T(8,128)S(1)} %get-tuple-element.47), channel_id=1, source_target_pairs={{8,16},{10,18},{12,20},{14,22},{16,8},{18,10},{20,12},{22,14},{0,2... | collective-permute-start | bytes 270344 | tf_op jit(solution)/shard_map/ppermute | solution.py:940
  15.4 3.3 %copy-start.1 = (bf16[4,3,4,64,128]{4,3,2,1,0:T(8,128)(2,1)S(1)}, bf16[4,3,4,64,128]{4,3,2,1,0:T(8,128)(2,1)}, u32[]{:S(2)}) copy-start(bf16[4,3,4,64,128]{4,3,2,1,0:T(8,128)(2,1)} %forward.1) | copy-start | bytes 2359300

commit v5 on v3

--- a/solution.py
+++ b/solution.py
@@ -150,7 +150,7 @@
         out[1, here, :] = jnp.where(even, low, high)
 
 
-def x_unpack_kernel(from_a, from_b, partly, halo, out):
+def x_unpack_kernel(from_b, from_a, partly, halo, out):
     depth = (halo.shape[0] - 1) // 7
     lanes = halo.shape[2]
     even = is_even("gx")
@@ -832,8 +832,8 @@
         name="x_pack",
     )
     swap_a, swap_b = swaps(lax.axis_size("gx"), True)
+    from_b = lax.ppermute(to_b, "gx", swap_b)
     from_a = lax.ppermute(to_a, "gx", swap_a)
-    from_b = lax.ppermute(to_b, "gx", swap_b)
 
     pairs_a, z_a, pairs_b, z_b = z_swaps(lax.axis_size("gz"), lax.axis_size("gx"))
     with_coef = [sends_coef(depth, lax.axis_size("gz"), pairs) for pairs in (pairs_a, pairs_b)]
@@ -849,7 +849,7 @@
     )
     halo, y_out = call(
         x_unpack_kernel,
-        [from_a, from_b, partly],
+        [from_b, from_a, partly],
         [(slabs, TILE, lanes), (2, wide, lanes)],
         aliases={2: 1},
         name="x_unpack",

time: 21.9 us -> 21.8 us (level)
  waiting for transfers between devices: 3.14 us -> 2.57 us
  starting transfers between devices: 9.56 us -> 10.1 us
    ppermute x1, starting transfers between devices: 1.47 us -> 2.43 us  [on_device(): both = lax.ppermute(y_out, 'gy', swap_a)]
    ppermute x1, waiting for transfers between devices: 0.61 us -> 0.1 us  [on_device(): from_b = lax.ppermute(to_b, 'gx', swap_b)]
    ppermute x1, starting transfers between devices: 2.58 us -> 2.17 us  [on_device(): early_a = lax.ppermute(early_a, ('gz', 'gx'), z_a)]
where the time goes in v5:
time: 21.8 us; the launch traced here: 21.6 us
  starting transfers between devices  10.1 us (46%)
  Pallas kernels  7.61 us (35%)
  waiting for transfers between devices  2.57 us (12%)
  between operations  1.39 us (6%)
    pallas_call x8, Pallas kernels, call(): pl.pallas_call(kernel, out_shape=[jax.ShapeDtypeStruct(s, F32) for s in o...  7.61 us
    ppermute x1, starting transfers between devices, on_device(): from_b = lax.ppermute(to_b, 'gx', swap_b)  2.47 us
    ppermute x1, waiting for transfers between devices, on_device(): late_a = lax.ppermute(late_a, ('gz', 'gx'), z_a)  2.46 us
    ppermute x1, starting transfers between devices, on_device(): both = lax.ppermute(y_out, 'gy', swap_a)  2.43 us
    ppermute x1, starting transfers between devices, on_device(): late_a = lax.ppermute(late_a, ('gz', 'gx'), z_a)  2.23 us
    ppermute x1, starting transfers between devices, on_device(): early_a = lax.ppermute(early_a, ('gz', 'gx'), z_a)  2.17 us
    ppermute x1, starting transfers between devices, on_device(): from_a = lax.ppermute(to_a, 'gx', swap_a)  0.68 us
  transfers between devices with their start and end apart: 7, of which 2 were waited for; matrix products, arithmetic and copies ran while one was open for 0% of the time, Pallas kernels for 16%

profile of v5, /device:TPU:0, one launch (start us, length us, event | category | flops | bytes accessed | tf_op | source)
XLA Modules:
  0.0 21.6 jit_solution(16240692050580038980)
XLA Ops:
  0.6 0.0 copy-start
  0.6 1.2 %x_pack.1 = (f32[15,8,128]{2,1,0:T(8,128)S(1)}, f32[15,8,128]{2,1,0:T(8,128)S(1)}, f32[8,128]{1,0:T(8,128)S(1)}, s32[4,64,128]{2,1,0:T(8,128)S(1)}, f32[64,128]{1,0:T(8,128)S(1)}) custom-call(f32[6,4,64,128]{3,2,1,0:T(8,128)} %fields.11, s32[4,64,128]{2,1,0:T(8,128)} %material.1, f32[64,128]{1,0:T(8,128)} %profile.1, f32[4]{0:T(128)} %eps.1, f32[4]{0:T(128)} %wave.1), custom_call_target="tpu_custom_call" | custom-call | tf_op jit(solution)/shard_map/x_pack/pallas_call | solution.py:795
  1.8 2.5 %collective-permute-start = (f32[15,8,128]{2,1,0:T(8,128)S(1)}, f32[15,8,128]{2,1,0:T(8,128)S(1)}, u32[]{:S(2)}, u32[]{:S(2)}) collective-permute-start(f32[15,8,128]{2,1,0:T(8,128)S(1)} %get-tuple-element.25), channel_id=1, source_target_pairs={{2,4},{6,0},{4,2},{0,6},{3,5},{7,1},{5,3},{1,7},{10,12},{14,8},{12... | collective-permute-start | bytes 184328 | tf_op jit(solution)/shard_map/ppermute | solution.py:835
  4.3 0.7 %collective-permute-start.1 = (f32[15,8,128]{2,1,0:T(8,128)S(1)}, f32[15,8,128]{2,1,0:T(8,128)S(1)}, u32[]{:S(2)}, u32[]{:S(2)}) collective-permute-start(f32[15,8,128]{2,1,0:T(8,128)S(1)} %get-tuple-element.26), channel_id=1, source_target_pairs={{0,2},{4,6},{2,0},{6,4},{1,3},{5,7},{3,1},{7,5},{8,10},{12,14},{10... | collective-permute-start | bytes 184328 | tf_op jit(solution)/shard_map/ppermute | solution.py:836
  5.6 0.0 copy-done
  5.7 0.9 %interior.1 = (f32[4,64,128]{2,1,0:T(8,128)S(1)}, f32[488,128]{1,0:T(8,128)S(1)}, f32[616,128]{1,0:T(8,128)S(1)}, f32[2,72,128]{2,1,0:T(8,128)S(1)}, f32[28,128]{1,0:T(8,128)S(1)}) custom-call(f32[6,4,64,128]{3,2,1,0:T(8,128)S(1)} %copy-done, s32[4,64,128]{2,1,0:T(8,128)S(1)} %get-tuple-element.21.material, f32[64,128]{1,0:T(8,128)S(1)} %get-tuple-element.22.profile, ...), custom_call_target="tpu_custom_call" | custom-call | tf_op jit(solution)/shard_map/interior/pallas_call | solution.py:795
  6.5 0.1 collective-permute-start.3
  6.6 0.1 collective-permute-done.from_b
  6.7 0.0 collective-permute-done.1.from_a
  6.7 0.1 x_unpack.1
  6.8 2.4 %collective-permute-start.2 = (f32[2,72,128]{2,1,0:T(8,128)S(1)}, f32[2,72,128]{2,1,0:T(8,128)S(1)}, u32[]{:S(2)}, u32[]{:S(2)}) collective-permute-start(f32[2,72,128]{2,1,0:T(8,128)S(1)} %get-tuple-element.30), channel_id=1, source_target_pairs={{0,1},{1,0},{2,3},{3,2},{4,5},{5,4},{6,7},{7,6},{8,9},{9,8},{10,11... | collective-permute-start | bytes 221192 | tf_op jit(solution)/shard_map/ppermute | solution.py:859
  9.2 2.2 %collective-permute-start.4 = (f32[488,128]{1,0:T(8,128)S(1)}, f32[488,128]{1,0:T(8,128)S(1)}, u32[]{:S(2)}, u32[]{:S(2)}) collective-permute-start(f32[488,128]{1,0:T(8,128)S(1)} %get-tuple-element.36), channel_id=1, source_target_pairs={{0,8},{2,10},{4,12},{6,14},{16,24},{18,26},{20,28},{22,30},{8,0},{... | collective-permute-start | bytes 749576 | tf_op jit(solution)/shard_map/ppermute | solution.py:865
  11.4 0.7 %own_strips.1.own = f32[8,72,128]{2,1,0:T(8,128)S(1)} custom-call(f32[6,4,64,128]{3,2,1,0:T(8,128)S(1)} %copy-done, f32[4,64,128]{2,1,0:T(8,128)S(1)} %get-tuple-element.24.coef, f32[64,128]{1,0:T(8,128)S(1)} %get-tuple-element.22.profile, f32[29,8,128]{2,1,0:T(8,128)S(1)} %get-tuple-element.28.halo), custom_call_target="tpu_custom_call" | custom-call | tf_op jit(solution)/shard_map/own_strips/pallas_call | solution.py:795
  12.1 0.0 collective-permute-done.2
  12.1 1.0 %frame.1 = (f32[8,72,128]{2,1,0:T(8,128)S(1)}, f32[136,128]{1,0:T(8,128)S(1)}, f32[176,128]{1,0:T(8,128)S(1)}) custom-call(f32[6,4,64,128]{3,2,1,0:T(8,128)S(1)} %copy-done, f32[4,64,128]{2,1,0:T(8,128)S(1)} %get-tuple-element.24.coef, f32[64,128]{1,0:T(8,128)S(1)} %get-tuple-element.22.profile, f32[28,128]{1,0:T(8,128)S(1)} %get-tuple-element.29.table, ...), custom_call_target="tpu_custom_call" | custom-call | tf_op jit(solution)/shard_map/frame/pallas_call | solution.py:795
  13.1 2.2 %collective-permute-start.5 = (f32[136,128]{1,0:T(8,128)S(1)}, f32[136,128]{1,0:T(8,128)S(1)}, u32[]{:S(2)}, u32[]{:S(2)}) collective-permute-start(f32[136,128]{1,0:T(8,128)S(1)} %get-tuple-element.38), channel_id=1, source_target_pairs={{0,8},{2,10},{4,12},{6,14},{16,24},{18,26},{20,28},{22,30},{8,0},{... | collective-permute-start | bytes 208904 | tf_op jit(solution)/shard_map/ppermute | solution.py:882
  15.3 0.0 collective-permute-start.6
  15.3 0.0 collective-permute-done.3.refs_0_
  15.3 0.8 %prepare.1 = (f32[8,72,128]{2,1,0:T(8,128)S(1)}, f32[3,6,72,128]{3,2,1,0:T(8,128)S(1)}, f32[2,4,72,128]{3,2,1,0:T(8,128)S(1)}, f32[616,128]{1,0:T(8,128)S(1)}) custom-call(f32[6,4,64,128]{3,2,1,0:T(8,128)S(1)} %copy-done, f32[29,8,128]{2,1,0:T(8,128)S(1)} %get-tuple-element.28.halo, ...), custom_call_target="tpu_custom_call", output_to_operand_aliasing={{3}: (3, {})} | custom-call | tf_op jit(solution)/shard_map/prepare/pallas_call | solution.py:795
  16.1 2.5 %collective-permute-done.5.late_a = f32[136,128]{1,0:T(8,128)S(1)} collective-permute-done((f32[136,128]{1,0:T(8,128)S(1)}, f32[136,128]{1,0:T(8,128)S(1)}, u32[]{:S(2)}, u32[]{:S(2)}) %collective-permute-start.5) | collective-permute-done | bytes 69664 | tf_op jit(solution)/shard_map/ppermute | solution.py:882
  18.6 0.0 collective-permute-done.6.late_b
  18.6 0.0 collective-permute-done.4.early_a
  18.6 0.0 copy-done.1
  18.6 3.1 %window.1 = (f32[6,4,64,128]{3,2,1,0:T(8,128)}, f32[4,64,128]{2,1,0:T(8,128)}) custom-call(f32[6,4,64,128]{3,2,1,0:T(8,128)S(1)} %copy-done, f32[4,64,128]{2,1,0:T(8,128)S(1)} %get-tuple-element.24.coef, f32[64,128]{1,0:T(8,128)S(1)} %get-tuple-element.22.profile, f32[29,8,128]{2,1,0:T(8,128)S(1)} %get-tuple-element.28.halo, ...), custom_call_target="tpu_custom_call" | custom-call | tf_op jit(solution)/shard_map/window/pallas_call | solution.py:795
  (4 shorter events, 0.0 us)
Async XLA Ops:
  0.6 5.0 %copy-start = (f32[6,4,64,128]{3,2,1,0:T(8,128)S(1)}, f32[6,4,64,128]{3,2,1,0:T(8,128)}, u32[]{:S(2)}) copy-start(f32[6,4,64,128]{3,2,1,0:T(8,128)} %fields.11) | copy-start | bytes 2359300
  1.8 4.9 %collective-permute-start = (f32[15,8,128]{2,1,0:T(8,128)S(1)}, f32[15,8,128]{2,1,0:T(8,128)S(1)}, u32[]{:S(2)}, u32[]{:S(2)}) collective-permute-start(f32[15,8,128]{2,1,0:T(8,128)S(1)} %get-tuple-element.25), channel_id=1, source_target_pairs={{2,4},{6,0},{4,2},{0,6},{3,5},{7,1},{5,3},{1,7},{10,12},{14,8},{12... | collective-permute-start | bytes 184328 | tf_op jit(solution)/shard_map/ppermute | solution.py:835
  4.3 2.4 %collective-permute-start.1 = (f32[15,8,128]{2,1,0:T(8,128)S(1)}, f32[15,8,128]{2,1,0:T(8,128)S(1)}, u32[]{:S(2)}, u32[]{:S(2)}) collective-permute-start(f32[15,8,128]{2,1,0:T(8,128)S(1)} %get-tuple-element.26), channel_id=1, source_target_pairs={{0,2},{4,6},{2,0},{6,4},{1,3},{5,7},{3,1},{7,5},{8,10},{12,14},{10... | collective-permute-start | bytes 184328 | tf_op jit(solution)/shard_map/ppermute | solution.py:836
  6.5 8.8 %collective-permute-start.3 = (f32[616,128]{1,0:T(8,128)S(1)}, f32[616,128]{1,0:T(8,128)S(1)}, u32[]{:S(2)}, u32[]{:S(2)}) collective-permute-start(f32[616,128]{1,0:T(8,128)S(1)} %get-tuple-element.32), channel_id=1, source_target_pairs={{8,16},{10,18},{12,20},{14,22},{16,8},{18,10},{20,12},{22,14},{0,2... | collective-permute-start | bytes 946184 | tf_op jit(solution)/shard_map/ppermute | solution.py:866
  6.8 5.3 %collective-permute-start.2 = (f32[2,72,128]{2,1,0:T(8,128)S(1)}, f32[2,72,128]{2,1,0:T(8,128)S(1)}, u32[]{:S(2)}, u32[]{:S(2)}) collective-permute-start(f32[2,72,128]{2,1,0:T(8,128)S(1)} %get-tuple-element.30), channel_id=1, source_target_pairs={{0,1},{1,0},{2,3},{3,2},{4,5},{5,4},{6,7},{7,6},{8,9},{9,8},{10,11... | collective-permute-start | bytes 221192 | tf_op jit(solution)/shard_map/ppermute | solution.py:859
  9.2 9.3 %collective-permute-start.4 = (f32[488,128]{1,0:T(8,128)S(1)}, f32[488,128]{1,0:T(8,128)S(1)}, u32[]{:S(2)}, u32[]{:S(2)}) collective-permute-start(f32[488,128]{1,0:T(8,128)S(1)} %get-tuple-element.36), channel_id=1, source_target_pairs={{0,8},{2,10},{4,12},{6,14},{16,24},{18,26},{20,28},{22,30},{8,0},{... | collective-permute-start | bytes 749576 | tf_op jit(solution)/shard_map/ppermute | solution.py:865
  13.1 5.5 %collective-permute-start.5 = (f32[136,128]{1,0:T(8,128)S(1)}, f32[136,128]{1,0:T(8,128)S(1)}, u32[]{:S(2)}, u32[]{:S(2)}) collective-permute-start(f32[136,128]{1,0:T(8,128)S(1)} %get-tuple-element.38), channel_id=1, source_target_pairs={{0,8},{2,10},{4,12},{6,14},{16,24},{18,26},{20,28},{22,30},{8,0},{... | collective-permute-start | bytes 208904 | tf_op jit(solution)/shard_map/ppermute | solution.py:882
  15.3 3.2 %collective-permute-start.6 = (f32[176,128]{1,0:T(8,128)S(1)}, f32[176,128]{1,0:T(8,128)S(1)}, u32[]{:S(2)}, u32[]{:S(2)}) collective-permute-start(f32[176,128]{1,0:T(8,128)S(1)} %get-tuple-element.39), channel_id=1, source_target_pairs={{8,16},{10,18},{12,20},{14,22},{16,8},{18,10},{20,12},{22,14},{0,2... | collective-permute-start | bytes 270344 | tf_op jit(solution)/shard_map/ppermute | solution.py:883
  15.3 3.2 %copy-start.1 = (bf16[4,3,4,64,128]{4,3,2,1,0:T(8,128)(2,1)S(1)}, bf16[4,3,4,64,128]{4,3,2,1,0:T(8,128)(2,1)}, u32[]{:S(2)}) copy-start(bf16[4,3,4,64,128]{4,3,2,1,0:T(8,128)(2,1)} %forward.1) | copy-start | bytes 2359300
